TPU v7x, 32 devices: a whole 2x2x4 slice. The times are simulated.
32 devices in a mesh: tm: 8 (over z, y), head: 4 (over x, core).
Axes of the slice: x: 2, y: 2, z: 4, core: 2. Of those that a mesh axis runs over, the one named last changes fastest.
Arguments:
- query: bfloat16 [1024, 3072], P(('tm', 'head')), may hold values from -100 to 100
- key_cur: bfloat16 [1024, 3072], P(('tm', 'head')), may hold values from -6 to 6
- value_cur: bfloat16 [1024, 3072], P(('tm', 'head')), may hold values from -6 to 6
- d_out: bfloat16 [1024, 3072], P(('tm', 'head')), may hold values from -6 to 6
- key_hist: bfloat16 [2048, 3072], P('tm', 'head'), may hold values from -10 to 10
- value_hist: bfloat16 [2048, 3072], P('tm', 'head'), may hold values from -6 to 6
- hist_len: int32 [8], P('tm'), may hold values from 1 to 256, 1024 in all
Outputs:
- grad_query: bfloat16 [1024, 3072], P(('tm', 'head'))
- grad_key_cur: bfloat16 [1024, 3072], P(('tm', 'head'))
- grad_value_cur: bfloat16 [1024, 3072], P(('tm', 'head'))
- grad_key_hist: bfloat16 [2048, 3072], P('tm', 'head')
- grad_value_hist: bfloat16 [2048, 3072], P('tm', 'head')
Inputs may be any that keep to these rules, and one draw needn't show every extreme that they name: `hist_len`: every time shard has at least one filled slot; filled slots come first.
All inputs are finite; a program needn't handle non-finite values.
Results may differ from a plain program's by a relative error of at most 0.019.
Values may be sent and summed in bfloat16 or wider, within the bound.
A program may use at most 128 MiB of HBM per device.

v0:
```python
import math

import jax
import jax.numpy as jnp
from jax import lax
from jax.sharding import PartitionSpec as P

HS = 128


def block_stats(queries, grads, key_block, value_block, live_mask, score_scale):
    scores = (
        jnp.einsum("qhd,khd->hqk", queries, key_block, preferred_element_type=jnp.float32)
        * score_scale
    )
    row_max = jnp.max(jnp.where(live_mask, scores, -jnp.inf), axis=2)
    weights = jnp.where(live_mask, jnp.exp(scores - row_max[:, :, None]), 0.0)
    grad_scores = jnp.einsum("qhd,khd->hqk", grads, value_block, preferred_element_type=jnp.float32)
    return (row_max, jnp.sum(weights, axis=2), jnp.sum(weights * grad_scores, axis=2))


def prob_terms(
    queries, grads, key_block, value_block, live_mask, row_max, row_total, row_delta, score_scale
):
    scores = (
        jnp.einsum("qhd,khd->hqk", queries, key_block, preferred_element_type=jnp.float32)
        * score_scale
    )
    grad_scores = jnp.einsum("qhd,khd->hqk", grads, value_block, preferred_element_type=jnp.float32)
    full_prob = jnp.where(
        live_mask, jnp.exp(scores - row_max[:, :, None]) / row_total[:, :, None], 0.0
    )
    score_grad = (score_scale * full_prob * (grad_scores - row_delta[:, :, None])).astype(
        jnp.bfloat16
    )
    return (full_prob.astype(jnp.bfloat16), score_grad)


def shards(query, key_cur, value_cur, d_out, key_hist, value_hist, hist_len):
    local_query, local_key, local_value, local_grad = (
        lax.all_to_all(query, "head", split_axis=1, concat_axis=0, tiled=True),
        lax.all_to_all(key_cur, "head", split_axis=1, concat_axis=0, tiled=True),
        lax.all_to_all(value_cur, "head", split_axis=1, concat_axis=0, tiled=True),
        lax.all_to_all(d_out, "head", split_axis=1, concat_axis=0, tiled=True),
    )
    row_count = local_query.shape[0]
    feat_width = local_query.shape[1]
    head_count = feat_width // HS
    score_scale = 1.0 / math.sqrt(HS)
    own_keys = jnp.concatenate([local_key, key_hist], axis=0).reshape(-1, head_count, HS)
    own_values = jnp.concatenate([local_value, value_hist], axis=0).reshape(-1, head_count, HS)
    key_count = own_keys.shape[0]
    slot_index = jnp.arange(key_count)
    query_heads = local_query.reshape(row_count, head_count, HS)
    grad_heads = local_grad.reshape(row_count, head_count, HS)

    def live_of(filled):
        return (slot_index < row_count) | (slot_index - row_count < filled)

    gathered_keys, gathered_values, hist_counts = (
        lax.all_gather(own_keys, "tm", axis=0, tiled=True),
        lax.all_gather(own_values, "tm", axis=0, tiled=True),
        lax.all_gather(hist_len, "tm", axis=0, tiled=True),
    )
    block_count = hist_counts.shape[0]

    def key_slice(block_id):
        start_row = block_id * key_count
        return (
            lax.dynamic_slice_in_dim(gathered_keys, start_row, key_count, 0),
            lax.dynamic_slice_in_dim(gathered_values, start_row, key_count, 0),
            live_of(hist_counts[block_id]),
        )

    def stat_block(block_id):
        key_block, value_block, live_mask = key_slice(block_id)
        return block_stats(query_heads, grad_heads, key_block, value_block, live_mask, score_scale)

    block_max, block_total, block_dots = lax.map(stat_block, jnp.arange(block_count))
    row_max = jnp.max(block_max, axis=0)
    rescale = jnp.exp(block_max - row_max[None])
    row_total = jnp.sum(block_total * rescale, axis=0)
    row_delta = jnp.sum(block_dots * rescale, axis=0) / row_total

    def add_query(accum, block_id):
        key_block, value_block, live_mask = key_slice(block_id)
        prob_low, score_grad = prob_terms(
            query_heads,
            grad_heads,
            key_block,
            value_block,
            live_mask,
            row_max,
            row_total,
            row_delta,
            score_scale,
        )
        return (
            accum
            + jnp.einsum("hqk,khd->qhd", score_grad, key_block, preferred_element_type=jnp.float32),
            None,
        )

    summed_query, _ = lax.scan(
        add_query, jnp.zeros((row_count, head_count, HS), jnp.float32), jnp.arange(block_count)
    )
    grad_query = summed_query.reshape(row_count, feat_width)

    def block_terms(inner_id):
        key_block, value_block, live_mask = key_slice(inner_id)
        prob_low, score_grad = prob_terms(
            query_heads,
            grad_heads,
            key_block,
            value_block,
            live_mask,
            row_max,
            row_total,
            row_delta,
            score_scale,
        )
        grad_k = jnp.einsum(
            "hqk,qhd->khd", score_grad, query_heads, preferred_element_type=jnp.float32
        )
        grad_v = jnp.einsum(
            "hqk,qhd->khd", prob_low, grad_heads, preferred_element_type=jnp.float32
        )
        return jnp.concatenate(
            [grad_k.reshape(key_count, feat_width), grad_v.reshape(key_count, feat_width)], axis=1
        )

    summed_keys = lax.psum_scatter(
        lax.map(block_terms, jnp.arange(key_count * lax.axis_size("tm") // key_count))
        .reshape(key_count * lax.axis_size("tm"), 2 * feat_width)
        .astype(jnp.bfloat16),
        "tm",
        scatter_dimension=0,
        tiled=True,
    ).astype(jnp.float32)
    grad_keys = summed_keys[:, :feat_width]
    grad_values = summed_keys[:, feat_width:]
    query_low = grad_query.astype(jnp.bfloat16)
    keys_low = grad_keys.astype(jnp.bfloat16)
    values_low = grad_values.astype(jnp.bfloat16)
    back_query, back_key, back_value = (
        lax.all_to_all(query_low, "head", split_axis=0, concat_axis=1, tiled=True),
        lax.all_to_all(keys_low[:row_count], "head", split_axis=0, concat_axis=1, tiled=True),
        lax.all_to_all(values_low[:row_count], "head", split_axis=0, concat_axis=1, tiled=True),
    )
    return (back_query, back_key, back_value, keys_low[row_count:], values_low[row_count:])


def solution(mesh):
    in_specs = (
        P(("tm", "head"), None),
        P(("tm", "head"), None),
        P(("tm", "head"), None),
        P(("tm", "head"), None),
        P("tm", "head"),
        P("tm", "head"),
        P("tm"),
    )
    out_specs = (
        P(("tm", "head"), None),
        P(("tm", "head"), None),
        P(("tm", "head"), None),
        P("tm", "head"),
        P("tm", "head"),
    )
    return jax.shard_map(shards, mesh=mesh, in_specs=in_specs, out_specs=out_specs, check_vma=False)
```

profile of v0, /device:TPU:0, one launch (start us, length us, event | category | flops | bytes accessed | tf_op | source)
XLA Modules:
  0.0 524.1 jit_solution(17317554499413578613)
XLA Ops:
  7.2 1.6 copy.120
  8.8 4.2 all-to-all-start
  14.2 4.2 all-to-all-done
  20.4 3.4 all-to-all-start.2
  24.1 5.1 all-to-all-done.2
  31.2 3.4 all-to-all-start.1
  35.3 4.6 all-to-all-done.1
  39.9 3.4 all-to-all-start.3
  45.3 12.2 %all-reduce = s32[8]{0:T(128)S(1)} all-reduce(s32[8]{0:T(128)S(1)} %dynamic-update-slice), channel_id=1, replica_groups=mesh['tm'=8,'head'=4] {'tm'}, use_global_device_ids=true, to_apply=%add | all-reduce | flops 8 | bytes 64
  58.5 43.4 %all-gather.3.cloned.1.call-done = bf16[3072,6,128]{0,2,1:T(8,128)(2,1)} async-done(((bf16[384,6,128]{0,2,1:T(8,128)(2,1)}), bf16[3072,6,128]{0,2,1:T(8,128)(2,1)}) %all-gather.3.cloned.1.call-update) | async-done | bytes 4718608 | tf_op jit(solution)/shard_map/all_gather | solution.py:61
  101.9 6.6 %copy.90 = bf16[3072,6,128]{2,0,1:T(8,128)(2,1)} copy(bf16[3072,6,128]{0,2,1:T(8,128)(2,1)} %all-gather.3.cloned.1.call-done) | data formatting | bytes 9437184
  108.5 74.7 %all-gather.5.cloned.1.call-done = bf16[3072,6,128]{0,2,1:T(8,128)(2,1)} async-done(((bf16[384,6,128]{0,2,1:T(8,128)(2,1)}), bf16[3072,6,128]{0,2,1:T(8,128)(2,1)}) %all-gather.5.cloned.1.call-update) | async-done | bytes 4718608 | tf_op jit(solution)/shard_map/all_gather | solution.py:62
  183.2 6.7 %copy.88 = bf16[3072,6,128]{2,0,1:T(8,128)(2,1)} copy(bf16[3072,6,128]{0,2,1:T(8,128)(2,1)} %all-gather.5.cloned.1.call-done) | data formatting | bytes 9437184
  189.9 60.5 %while.46 = (s32[]{:T(128)}, f32[8,6,128]{2,1,0:T(8,128)S(1)}, f32[8,6,128]{2,1,0:T(8,128)S(1)}, f32[8,6,128]{2,1,0:T(8,128)S(1)}, s32[8]{0:T(128)S(1)}, /*index...) while((s32[]{:T(128)}, f32[8,6,128]{2,1,0:T(8,128)S(1)}, ...), condition=%wide.region_4.5_spmd.clone.clone, body=%wide.region_0.4_spmd.clone.clone.sunk | while | flops 153943296 | bytes 5153553 | solution.py:79
  195.7 1.4 fusion.95
  203.3 1.5 fusion.95
  210.9 1.5 fusion.95
  218.4 1.5 fusion.95
  226.0 1.5 fusion.95
  233.6 1.5 fusion.95
  241.1 1.5 fusion.95
  248.7 1.5 fusion.95
  250.5 72.9 %while.47 = (s32[]{:T(128)}, bf16[8,384,1536]{1,2,0:T(8,128)(2,1)}, s32[8]{0:T(128)S(1)}, s32[8]{0:T(128)S(1)}, bf16[3072,6,128]{2,0,1:T(8,128)(2,1)}, /*index=5...) while((s32[]{:T(128)}, bf16[8,384,1536]{1,2,0:T(8,128)(2,1)}, ...), condition=%wide.region_11.12_spmd.clone.clone, body=%wide.region_10.11_spmd.clone.clone.sunk | while | flops 307004928 | bytes 9054229 | solution.py:133
  254.9 1.5 fusion.104
  256.4 1.6 fusion.106
  264.0 1.5 fusion.104
  265.5 1.6 fusion.106
  273.1 1.5 fusion.104
  274.6 1.6 fusion.106
  282.2 1.5 fusion.104
  283.7 1.6 fusion.106
  291.3 1.5 fusion.104
  292.8 1.6 fusion.106
  300.4 1.5 fusion.104
  301.9 1.6 fusion.106
  309.5 1.5 fusion.104
  311.0 1.6 fusion.106
  318.6 1.5 fusion.104
  320.1 1.6 fusion.106
  323.4 12.6 %copy.100 = bf16[8,384,1536]{2,1,0:T(8,128)(2,1)} copy(bf16[8,384,1536]{1,2,0:T(8,128)(2,1)} %get-tuple-element.455) | data formatting | bytes 18874368 | tf_op jit(solution)/shard_map/convert_element_type | solution.py:135
  336.0 63.0 %while.48 = (s32[]{:T(128)}, f32[128,6,128]{0,2,1:T(8,128)S(1)}, s32[8]{0:T(128)S(1)}, bf16[3072,6,128]{2,0,1:T(8,128)(2,1)}, s32[8]{0:T(128)S(1)}, /*index=5*/b...) while((s32[]{:T(128)}, f32[128,6,128]{0,2,1:T(8,128)S(1)}, ...), condition=%wide.region_9.10_spmd.clone.clone, body=%wide.region_8.9_spmd.clone.clone.sunk | while | flops 229049856 | bytes 5320214 | solution.py:104
  340.5 1.7 fusion.114
  342.1 1.9 fusion.115
  348.5 1.5 fusion.114
  350.0 1.8 fusion.115
  356.3 1.5 fusion.114
  357.8 1.8 fusion.115
  364.1 1.5 fusion.114
  365.7 1.8 fusion.115
  372.0 1.5 fusion.114
  373.5 1.8 fusion.115
  379.8 1.5 fusion.114
  381.4 1.9 fusion.115
  387.7 1.6 fusion.114
  389.3 1.8 fusion.115
  395.6 1.5 fusion.114
  397.1 1.9 fusion.115
  400.2 3.4 all-to-all-start.4
  403.5 94.1 %reduce-scatter.2.cloned.1.call-done = bf16[384,1536]{1,0:T(8,128)(2,1)} async-done(((bf16[3072,1536]{1,0:T(8,128)(2,1)}), bf16[384,1536]{1,0:T(8,128)(2,1)}) %reduce-scatter.2.cloned.1.call-update) | async-done | bytes 1179664 | tf_op jit(solution)/shard_map/reduce_scatter | solution.py:132
  497.7 1.9 fusion.57
  499.6 3.4 all-to-all-start.5
  503.6 4.6 all-to-all-done.5
  508.2 3.4 all-to-all-start.6
  513.2 3.7 all-to-all-done.6
  (178 shorter events, 82.1 us)
Async XLA Ops:
  8.8 9.5 %all-to-all-start = ((bf16[32,4,768]{2,0,1:T(8,128)(2,1)}), bf16[32,4,768]{2,0,1:T(8,128)(2,1)S(1)}, u32[]{:S(2)}, u32[]{:S(2)}) async-start(bf16[32,4,768]{2,0,1:T(8,128)(2,1)} %bitcast.77), calls=%async_computation | async-start | bytes 393216 | tf_op jit(solution)/shard_map/all_to_all | solution.py:42
  13.0 88.9 %all-gather.3.cloned.1.call-start = ((), (), s32[]{:S(2)}) async-start(), calls=%async_computation.8 | async-start | bytes 5308416 | tf_op jit(solution)/shard_map/all_gather | solution.py:61
  18.6 1.2 copy-start.2
  18.8 5.1 copy-start.1
  20.4 8.7 %all-to-all-start.2 = ((bf16[32,4,768]{2,0,1:T(8,128)(2,1)}), bf16[32,4,768]{2,0,1:T(8,128)(2,1)S(1)}, u32[]{:S(2)}, u32[]{:S(2)}) async-start(bf16[32,4,768]{2,0,1:T(8,128)(2,1)} %bitcast.75), calls=%async_computation.2 | async-start | bytes 393216 | tf_op jit(solution)/shard_map/all_to_all | solution.py:43
  23.8 159.4 %all-gather.5.cloned.1.call-start = ((), (), s32[]{:S(2)}) async-start(), calls=%async_computation.9 | async-start | bytes 5308416 | tf_op jit(solution)/shard_map/all_gather | solution.py:62
  29.4 1.2 copy-start.3
  29.6 5.0 copy-start.4
  30.5 13.5 %copy-start.5 = (u32[32]{0:T(128)S(1)}, u32[32]{0:T(128)}, u32[]{:S(2)}) copy-start(u32[32]{0:T(128)} %constant.167) | copy-start | bytes 388
  31.2 8.7 %all-to-all-start.1 = ((bf16[32,4,768]{2,0,1:T(8,128)(2,1)}), bf16[32,4,768]{2,0,1:T(8,128)(2,1)S(1)}, u32[]{:S(2)}, u32[]{:S(2)}) async-start(bf16[32,4,768]{2,0,1:T(8,128)(2,1)} %bitcast.76), calls=%async_computation.1 | async-start | bytes 393216 | tf_op jit(solution)/shard_map/all_to_all | solution.py:41
  39.9 18.1 %all-to-all-start.3 = ((bf16[32,4,768]{2,0,1:T(8,128)(2,1)}), bf16[32,4,768]{2,0,1:T(8,128)(2,1)S(1)}, u32[]{:S(2)}, u32[]{:S(2)}) async-start(bf16[32,4,768]{2,0,1:T(8,128)(2,1)} %bitcast.74), calls=%async_computation.3 | async-start | bytes 393216 | tf_op jit(solution)/shard_map/all_to_all | solution.py:44
  43.3 454.4 %reduce-scatter.2.cloned.1.call-start = ((), (), s32[]{:S(2)}) async-start(), calls=%async_computation.10 | async-start | bytes 10616832 | tf_op jit(solution)/shard_map/reduce_scatter | solution.py:132
  400.2 99.4 %all-to-all-start.4 = ((bf16[4,32,768]{2,1,0:T(8,128)(2,1)}), bf16[4,32,768]{2,1,0:T(8,128)(2,1)S(1)}, u32[]{:S(2)}, u32[]{:S(2)}) async-start(bf16[4,32,768]{2,1,0:T(8,128)(2,1)} %convert_element_type.35), calls=%async_computation.4 | async-start | bytes 393216 | tf_op jit(solution)/shard_map/all_to_all | solution.py:146
  497.7 13.9 %copy-start = (bf16[384,1536]{1,0:T(8,128)(2,1)S(1)}, bf16[384,1536]{1,0:T(8,128)(2,1)}, u32[]{:S(2)}) copy-start(bf16[384,1536]{1,0:T(8,128)(2,1)} %reduce-scatter.2.cloned.1.call-done) | copy-start | bytes 3538948
  499.6 8.7 %all-to-all-start.5 = ((bf16[4,32,768]{2,1,0:T(8,128)(2,1)}), bf16[4,32,768]{2,1,0:T(8,128)(2,1)S(1)}, u32[]{:S(2)}, u32[]{:S(2)}) async-start(bf16[4,32,768]{2,1,0:T(8,128)(2,1)} %bitcast.9), calls=%async_computation.6 | async-start | bytes 393216 | tf_op jit(solution)/shard_map/all_to_all | solution.py:147
  508.2 8.7 %all-to-all-start.6 = ((bf16[4,32,768]{2,1,0:T(8,128)(2,1)}), bf16[4,32,768]{2,1,0:T(8,128)(2,1)S(1)}, u32[]{:S(2)}, u32[]{:S(2)}) async-start(bf16[4,32,768]{2,1,0:T(8,128)(2,1)} %bitcast.11), calls=%async_computation.7 | async-start | bytes 393216 | tf_op jit(solution)/shard_map/all_to_all | solution.py:148
Sparse Core Ops, SparseCore 0:
  19.9 81.9 all-gather.2
  104.0 79.1 all-gather.4
  336.1 161.4 reduce-scatter.1
where the time goes:
time: 529 us; the launch traced here: 524 us
  waiting for transfers between devices  234 us (44%)
  matrix products  78 us (15%)
  local copies, waits for them, and re-layouts  68.4 us (13%)
  loops' own time  63.3 us (12%)
  other arithmetic  28.7 us (5%)
  starting transfers between devices  24.5 us (5%)
  between operations  14.7 us (3%)
  blocking collectives  12.2 us (2%)
    reduce_scatter x1, waiting for transfers between devices, shards(): lax.psum_scatter(lax.map(block_terms, jnp.arange(key_count * lax.axis_siz...  94.1 us
    all_gather x1, waiting for transfers between devices, shards(): lax.all_gather(own_values, 'tm', axis=0, tiled=True)  74.7 us
    all_gather x1, waiting for transfers between devices, shards(): lax.all_gather(own_keys, 'tm', axis=0, tiled=True)  43.4 us
    dot_general x16, matrix products, prob_terms(): jnp.einsum('qhd,khd->hqk', queries, key_block, preferred_element_type=jnp...  24.3 us
    another operation x1, loops' own time, shards(): lax.map(stat_block, jnp.arange(block_count))  21.2 us
    another operation x1, loops' own time, shards(): lax.scan(add_query, jnp.zeros((row_count, head_count, HS), jnp.float32),...  21.1 us
    another operation x1, loops' own time, shards(): lax.map(block_terms, jnp.arange(key_count * lax.axis_size('tm') // key_co...  21 us
    unnamed x23, local copies, waits for them, and re-layouts  16.5 us
  transfers between devices with their start and end apart: 10, of which 8 were waited for; matrix products, arithmetic and copies ran while one was open for 12% of the time, Pallas kernels for 0%

commit v1 on v0

v1 whole, which is shorter than its diff:
```python
import math

import jax
import jax.numpy as jnp
from jax import lax
from jax.sharding import PartitionSpec as P

HS = 128


def to_heads(x, axis_name="head"):
    return lax.all_to_all(x, axis_name, split_axis=1, concat_axis=0, tiled=True)


def shards(query, key_cur, value_cur, d_out, key_hist, value_hist, hist_len):
    n_head = lax.axis_size("head")
    rows, width = query.shape
    feat = width // n_head
    heads = feat // HS
    scale = 1.0 / math.sqrt(HS)

    both = jnp.stack([query, d_out], axis=0).reshape(2, rows, n_head, feat)
    both = lax.all_to_all(both, "head", split_axis=2, concat_axis=1, tiled=True)
    both = both.reshape(2, rows * n_head, feat)
    both = lax.all_gather(both, "tm", axis=1, tiled=True)
    queries, grads = both[0], both[1]
    n_q = queries.shape[0]

    kv = jnp.stack([key_cur, value_cur], axis=0).reshape(2, rows, n_head, feat)
    kv = lax.all_to_all(kv, "head", split_axis=2, concat_axis=1, tiled=True)
    kv = kv.reshape(2, rows * n_head, feat)
    cur = rows * n_head
    keys = jnp.concatenate([kv[0], key_hist], axis=0)
    values = jnp.concatenate([kv[1], value_hist], axis=0)
    n_k = keys.shape[0]

    def by_head(x):
        return x.reshape(x.shape[0], heads, HS).transpose(1, 0, 2)

    qh, gh, kh, vh = by_head(queries), by_head(grads), by_head(keys), by_head(values)
    slot = jnp.arange(n_k)
    live = (slot < cur) | (slot - cur < hist_len[0])
    s = jnp.einsum("hqd,hkd->hqk", qh, kh, preferred_element_type=jnp.float32) * scale
    g = jnp.einsum("hqd,hkd->hqk", gh, vh, preferred_element_type=jnp.float32)
    m = jnp.max(jnp.where(live, s, -jnp.inf), axis=2)
    w = jnp.where(live, jnp.exp(s - m[:, :, None]), 0.0)
    total = jnp.sum(w, axis=2)
    dots = jnp.sum(w * g, axis=2)
    stats = lax.all_gather(jnp.stack([m, total, dots]), "tm", axis=0, tiled=False)
    row_max = jnp.max(stats[:, 0], axis=0)
    back = jnp.exp(stats[:, 0] - row_max[None])
    row_total = jnp.sum(stats[:, 1] * back, axis=0)
    delta = jnp.sum(stats[:, 2] * back, axis=0) / row_total
    factor = jnp.exp(m - row_max) / row_total
    p = w * factor[:, :, None]
    prob = p.astype(jnp.bfloat16)
    sg = (scale * p * (g - delta[:, :, None])).astype(jnp.bfloat16)
    gq = jnp.einsum("hqk,hkd->qhd", sg, kh, preferred_element_type=jnp.float32)
    gq = gq.reshape(n_q, feat).astype(jnp.bfloat16)
    gq = lax.psum_scatter(gq, "tm", scatter_dimension=0, tiled=True)
    gk = jnp.einsum("hqk,hqd->khd", sg, qh, preferred_element_type=jnp.float32)
    gv = jnp.einsum("hqk,hqd->khd", prob, gh, preferred_element_type=jnp.float32)
    gk = gk.reshape(n_k, feat).astype(jnp.bfloat16)
    gv = gv.reshape(n_k, feat).astype(jnp.bfloat16)

    def to_tokens(x):
        return lax.all_to_all(x, "head", split_axis=0, concat_axis=1, tiled=True)

    return (to_tokens(gq), to_tokens(gk[:cur]), to_tokens(gv[:cur]), gk[cur:], gv[cur:])


def solution(mesh):
    tok, hist = P(("tm", "head"), None), P("tm", "head")
    return jax.shard_map(
        shards,
        mesh=mesh,
        in_specs=(tok, tok, tok, tok, hist, hist, P("tm")),
        out_specs=(tok, tok, tok, hist, hist),
        check_vma=False,
    )
```

time: 529 us -> 221 us (0.42)
  waiting for transfers between devices: 234 us -> 92.1 us
  loops' own time: 63.3 us -> 0 us
  matrix products: 78 us -> 18.1 us
  blocking collectives: 12.2 us -> 52.2 us
  local copies, waits for them, and re-layouts: 68.4 us -> 28.5 us
  other arithmetic: 28.7 us -> 4.1 us
  starting transfers between devices: 24.5 us -> 10.3 us
    all_gather x2 -> x1, waiting for transfers between devices: 118 us -> 45.9 us  [shards(): both = lax.all_gather(both, 'tm', axis=1, tiled=True)]
    another operation x3 -> x0, loops' own time: 63.3 us -> none  [the longest x1 21.2 us: shards(): lax.map(stat_block, jnp.arange(block_count))]
    dot_general x56 -> x5, matrix products: 78 us -> 18.1 us  [the longest x1 6.31 us: shards(): jnp.einsum('hqk,hqd->khd', prob, gh, preferred_element_type=jnp.float32)]
    reduce_scatter x1, waiting for transfers between devices: 94.1 us -> 39 us  [shards(): gq = lax.psum_scatter(gq, 'tm', scatter_dimension=0, tiled=True)]
    all_gather x0 -> x1, blocking collectives: none -> 32.3 us  [shards(): lax.all_gather(jnp.stack([m, total, dots]), 'tm', axis=0, tiled=False)]
    dynamic_slice x48 -> x0, local copies, waits for them, and re-layouts: 28.1 us -> none  [the longest x24 14.1 us: key_slice(): hist_counts[block_id]]
    all_to_all x0 -> x2, blocking collectives: none -> 19.8 us  [the longest x1 11.5 us: shards(): both = lax.all_to_all(both, 'head', split_axis=2, concat_axis=1, tiled=True)]
    or x24 -> x1, other arithmetic: 15.6 us -> 0.01 us  [shards(): live = (slot < cur) | (slot - cur < hist_len[0])]
  transfers between devices with their start and end apart: 10 -> 5, of which waited for: 8 -> 4; matrix products, arithmetic and copies ran while one was open for 12% -> 9% of each run, Pallas kernels for 0% -> 0%
where the time goes in v1:
time: 221 us; the launch traced here: 220 us
  waiting for transfers between devices  92.1 us (42%)
  blocking collectives  52.2 us (24%)
  local copies, waits for them, and re-layouts  28.5 us (13%)
  matrix products  18.1 us (8%)
  between operations  15.1 us (7%)
  starting transfers between devices  10.3 us (5%)
  other arithmetic  4.1 us (2%)
    all_gather x1, waiting for transfers between devices, shards(): both = lax.all_gather(both, 'tm', axis=1, tiled=True)  45.9 us
    reduce_scatter x1, waiting for transfers between devices, shards(): gq = lax.psum_scatter(gq, 'tm', scatter_dimension=0, tiled=True)  39 us
    all_gather x1, blocking collectives, shards(): lax.all_gather(jnp.stack([m, total, dots]), 'tm', axis=0, tiled=False)  32.3 us
    all_to_all x1, blocking collectives, shards(): both = lax.all_to_all(both, 'head', split_axis=2, concat_axis=1, tiled=True)  11.5 us
    all_to_all x1, blocking collectives, to_tokens(): return lax.all_to_all(x, 'head', split_axis=0, concat_axis=1, tiled=True)  8.38 us
    all_to_all x2, starting transfers between devices, to_tokens(): return lax.all_to_all(x, 'head', split_axis=0, concat_axis=1, tiled=True)  6.73 us
    dot_general x1, matrix products, shards(): jnp.einsum('hqk,hqd->khd', prob, gh, preferred_element_type=jnp.float32)  6.31 us
    slice x3, local copies, waits for them, and re-layouts, shards(): queries, grads = (both[0], both[1])  5.71 us
  transfers between devices with their start and end apart: 5, of which 4 were waited for; matrix products, arithmetic and copies ran while one was open for 9% of the time, Pallas kernels for 0%

profile of v1, /device:TPU:0, one launch (start us, length us, event | category | flops | bytes accessed | tf_op | source)
XLA Modules:
  0.0 220.4 jit_solution(3670029448561651911)
XLA Ops:
  7.2 0.0 copy-start.11
  7.2 0.0 copy-start.9
  7.2 0.0 all-gather.3.cloned.1.call-start
  7.2 1.1 stack.33
  8.4 1.1 stack.34
  9.4 0.3 pad_maximum_fusion.1
  9.8 11.5 %all_to_all.87 = bf16[2,32,4,768]{3,1,0,2:T(8,128)(2,1)S(1)} all-to-all(bf16[2,32,4,768]{3,1,0,2:T(8,128)(2,1)S(1)} %copy.111), channel_id=1, replica_groups=mesh['tm'=8,'head'=4] {'head'}, dimensions={2} | all-to-all | bytes 786432 | tf_op jit(solution)/shard_map/all_to_all | solution.py:23
  21.2 0.8 copy.112
  22.0 0.0 all-gather.3.cloned.1.call-update
  22.0 1.1 stack.30
  23.1 0.1 stack.31
  23.2 0.3 pad_maximum_fusion
  23.5 0.8 copy.107
  24.3 3.5 %all-to-all-start = ((bf16[2,32,4,768]{3,1,0,2:T(8,128)(2,1)}), bf16[2,32,4,768]{3,1,0,2:T(8,128)(2,1)S(1)}, u32[]{:S(2)}, u32[]{:S(2)}) async-start(bf16[2,32,4,768]{3,1,0,2:T(8,128)(2,1)} %copy.107), calls=%async_computation | async-start | bytes 786432 | tf_op jit(solution)/shard_map/all_to_all | solution.py:30
  27.8 0.0 reduce-scatter.2.cloned.1.call-start
  28.5 0.2 copy.108
  28.7 0.2 copy.110
  28.9 0.2 copy.117
  29.1 0.9 copy.119
  30.0 5.2 %all-to-all-done = bf16[2,32,4,768]{3,1,0,2:T(8,128)(2,1)S(1)} async-done(((bf16[2,32,4,768]{3,1,0,2:T(8,128)(2,1)}), bf16[2,32,4,768]{3,1,0,2:T(8,128)(2,1)S(1)}, u32[]{:S(2)}, u32[]{:S(2)}) %all-to-all-start) | async-done | bytes 393248 | tf_op jit(solution)/shard_map/all_to_all | solution.py:30
  35.2 0.2 concatenate.18
  35.5 0.7 copy.109
  36.2 0.2 concatenate.21
  36.4 0.7 copy.118
  37.1 45.9 %all-gather.3.cloned.1.call-done = bf16[2,1024,768]{2,1,0:T(8,128)(2,1)} async-done(((bf16[2,128,768]{2,1,0:T(8,128)(2,1)}), bf16[2,1024,768]{2,1,0:T(8,128)(2,1)}) %all-gather.3.cloned.1.call-update) | async-done | bytes 3145744 | tf_op jit(solution)/shard_map/all_gather | solution.py:25
  83.0 3.2 %fusion.21 = (bf16[1,1024,768]{2,1,0:T(8,128)(2,1)S(1)}, bf16[1,1024,768]{2,1,0:T(8,128)(2,1)}) fusion(bf16[2,1024,768]{2,1,0:T(8,128)(2,1)} %all-gather.3.cloned.1.call-done), kind=kLoop, calls=%fused_computation.40 | loop fusion | bytes 6291456 | tf_op jit(solution)/shard_map/slice | solution.py:26
  86.2 0.7 copy.113
  87.0 1.7 copy.115
  88.7 1.6 copy.116
  90.3 1.6 copy.114
  91.9 3.0 %select_reduce_fusion = (f32[6,1024]{1,0:T(8,128)S(1)}, f32[6,1024,384]{1,2,0:T(8,128)S(1)}) fusion(pred[384]{0:T(512)(128)(4,1)S(1)} %fusion.16, bf16[256,6,128]{2,0,1:T(8,128)(2,1)S(1)} %copy.110, bf16[128,6,128]{2,0,1:T(8,128)(2,1)} %copy.109, bf16[1024,6,128]{2,0,1:T(8,128)(2,1)} %copy.114), kind=kOutput, calls=%fused_computation.3 | convolution fusion | flops 612231168 | bytes 11624832 | tf_op jit(solution)/shard_map/hqd,hkd->hqk/dot_general | solution.py:43
  94.8 0.0 copy-start
  94.8 0.0 copy-start.6
  94.9 2.8 %fusion.20 = (f32[6,1024]{1,0:T(8,128)S(1)}, f32[6,1024]{1,0:T(8,128)S(1)}, f32[6,1024,384]{1,2,0:T(8,128)S(1)}) fusion(f32[6,1024]{1,0:T(8,128)S(1)} %get-tuple-element.40, f32[6,1024,384]{1,2,0:T(8,128)S(1)} %get-tuple-element.41, pred[384]{0:T(512)(128)(4,1)S(1)} %fusion.16, bf16[256,6,128]{2,0,1:T(8,128)(2,1)S(1)} %copy-done.5, ...), kind=kOutput, calls=%fused_computation.39 | convolution fusion | flops 619302912 | bytes 21111168 | tf_op jit(solution)/shard_map/hqd,hkd->hqk/dot_general | solution.py:44
  97.8 32.3 %all-gather = f32[24,6,1024]{2,1,0:T(8,128)S(1)} all-gather(f32[3,6,1024]{2,1,0:T(8,128)S(1)} %pad_maximum_fusion.2), channel_id=2, replica_groups=mesh['tm'=8,'head'=4] {'tm'}, dimensions={0}, use_global_device_ids=true | all-gather | bytes 663552 | tf_op jit(solution)/shard_map/all_gather | solution.py:49
  130.1 0.1 fusion.14
  130.2 0.0 copy-start.12
  130.3 0.0 copy-start.4
  130.3 3.4 %multiply_convert_fusion = bf16[6,1024,384]{1,2,0:T(8,128)(2,1)S(1)} fusion(f32[6,1024,384]{1,2,0:T(8,128)S(1)} %get-tuple-element.42, f32[6,1024]{1,0:T(8,128)S(1)} %get-tuple-element.39, f32[6,1024]{1,0:T(8,128)S(1)} %get-tuple-element.38, f32[6,1024]{1,0:T(8,128)S(1)} %get-tuple-element.40, f32[6,1024,384]{1,2,0:T(8,128)S(1)} %get-tuple-element.41, ...), kind=kLoop, calls=%fused_computation | loop fusion | flops 18874368 | bytes 23667072 | tf_op jit(solution)/shard_map/convert_element_type | solution.py:57
  133.7 2.2 %copy-done.1 = bf16[6,1024,384]{1,2,0:T(8,128)(2,1)} copy-done((bf16[6,1024,384]{1,2,0:T(8,128)(2,1)}, bf16[6,1024,384]{1,2,0:T(8,128)(2,1)S(1)}, u32[]{:S(2)}) %copy-start.1) | copy-done | bytes 4718616
  135.9 2.2 convolution_convert_fusion
  138.1 2.6 %copy.124 = bf16[1024,768]{1,0:T(8,128)(2,1)} copy(bf16[1024,768]{0,1:T(8,128)(2,1)} %bitcast.103) | data formatting | bytes 3145728 | tf_op jit(solution)/shard_map/convert_element_type | solution.py:59
  140.7 0.0 reduce-scatter.2.cloned.1.call-update
  140.7 3.8 %fusion.7 = bf16[384,6,128]{0,2,1:T(8,128)(2,1)S(1)} fusion(bf16[6,1024,128]{1,2,0:T(8,128)(2,1)S(1)} %bitcast.100, bf16[6,1024,384]{1,2,0:T(8,128)(2,1)} %copy-done.1), kind=kOutput, calls=%fused_computation.14 | convolution fusion | flops 604274688 | bytes 6881280 | tf_op jit(solution)/shard_map/hqk,hqd->khd/dot_general | solution.py:61
  144.6 0.8 copy-done.3
  145.4 0.2 copy.128
  145.6 0.9 all_to_all.74
  146.6 3.4 %all-to-all-start.3 = ((bf16[4,32,768]{2,1,0:T(8,128)(2,1)}), bf16[4,32,768]{2,1,0:T(8,128)(2,1)S(1)}, u32[]{:S(2)}, u32[]{:S(2)}) async-start(bf16[4,32,768]{2,1,0:T(8,128)(2,1)} %all_to_all.74), calls=%async_computation.4 | async-start | bytes 393216 | tf_op jit(solution)/shard_map/all_to_all | solution.py:67
  149.9 0.0 copy-done.7
  149.9 0.0 copy-done.13
  149.9 0.0 slice-start
  150.0 6.3 %fusion.8 = bf16[384,6,128]{0,2,1:T(8,128)(2,1)S(1)} fusion(bf16[6,1024,128]{1,2,0:T(8,128)(2,1)S(1)} %bitcast.102, f32[6,1024]{1,0:T(8,128)S(1)} %copy-done.13, f32[6,1024,384]{1,2,0:T(8,128)} %copy-done, f32[6,1024]{1,0:T(8,128)S(1)} %copy-done.7, pred[384]{0:T(512)(128)(4,1)S(1)} %fusion.16), kind=kOutput, calls=%fused_computation.15 | convolution fusion | flops 616071168 | bytes 11649408 | tf_op jit(solution)/shard_map/hqk,hqd->khd/dot_general | solution.py:62
  156.3 0.2 copy.132
  156.5 0.2 all_to_all.78
  156.8 0.0 all-to-all-done.3
  156.8 8.4 %all_to_all.88 = bf16[4,32,768]{2,1,0:T(8,128)(2,1)S(1)} all-to-all(bf16[4,32,768]{2,1,0:T(8,128)(2,1)S(1)} %all_to_all.78), channel_id=1, replica_groups=mesh['tm'=8,'head'=4] {'head'}, dimensions={0} | all-to-all | bytes 393216 | tf_op jit(solution)/shard_map/all_to_all | solution.py:67
  165.2 39.0 %reduce-scatter.2.cloned.1.call-done = bf16[128,768]{1,0:T(8,128)(2,1)} async-done(((bf16[1024,768]{1,0:T(8,128)(2,1)}), bf16[128,768]{1,0:T(8,128)(2,1)}) %reduce-scatter.2.cloned.1.call-update) | async-done | bytes 196624 | tf_op jit(solution)/shard_map/reduce_scatter | solution.py:60
  204.2 3.4 %all-to-all-start.2 = ((bf16[4,32,768]{2,1,0:T(8,128)(2,1)}), bf16[4,32,768]{2,1,0:T(8,128)(2,1)S(1)}, u32[]{:S(2)}, u32[]{:S(2)}) async-start(bf16[4,32,768]{2,1,0:T(8,128)(2,1)} %bitcast.116), calls=%async_computation.3 | async-start | bytes 393216 | tf_op jit(solution)/shard_map/all_to_all | solution.py:67
  207.6 0.9 copy.134
  208.5 0.9 copy.135
  209.4 0.7 copy.149
  210.1 0.7 copy.150
  210.8 2.0 all-to-all-done.2
  212.9 0.7 copy.148
  (28 shorter events, 0.3 us)
Async XLA Ops:
  7.2 15.9 %copy-start.11 = (bf16[32,3072]{1,0:T(8,128)(2,1)S(1)}, bf16[32,3072]{1,0:T(8,128)(2,1)}, u32[]{:S(2)}) copy-start(bf16[32,3072]{1,0:T(8,128)(2,1)} %param.9) | copy-start | bytes 589828
  7.2 21.3 %copy-start.9 = (bf16[256,768]{1,0:T(8,128)(2,1)S(1)}, bf16[256,768]{1,0:T(8,128)(2,1)}, u32[]{:S(2)}) copy-start(bf16[256,768]{1,0:T(8,128)(2,1)} %param.11) | copy-start | bytes 1179652
  7.2 21.7 %copy-start.10 = (bf16[256,768]{1,0:T(8,128)(2,1)S(1)}, bf16[256,768]{1,0:T(8,128)(2,1)}, u32[]{:S(2)}) copy-start(bf16[256,768]{1,0:T(8,128)(2,1)} %param.12) | copy-start | bytes 1179652
  7.2 75.8 %all-gather.3.cloned.1.call-start = ((), (), s32[]{:S(2)}) async-start(), calls=%async_computation.6 | async-start | bytes 3538944 | tf_op jit(solution)/shard_map/all_gather | solution.py:25
  24.3 10.9 %all-to-all-start = ((bf16[2,32,4,768]{3,1,0,2:T(8,128)(2,1)}), bf16[2,32,4,768]{3,1,0,2:T(8,128)(2,1)S(1)}, u32[]{:S(2)}, u32[]{:S(2)}) async-start(bf16[2,32,4,768]{3,1,0,2:T(8,128)(2,1)} %copy.107), calls=%async_computation | async-start | bytes 786432 | tf_op jit(solution)/shard_map/all_to_all | solution.py:30
  27.8 176.4 %reduce-scatter.2.cloned.1.call-start = ((), (), s32[]{:S(2)}) async-start(), calls=%async_computation.7 | async-start | bytes 1769472 | tf_op jit(solution)/shard_map/reduce_scatter | solution.py:60
  91.9 3.0 %copy-start.2 = (bf16[1024,6,128]{2,0,1:T(8,128)(2,1)S(1)}, bf16[1024,6,128]{2,0,1:T(8,128)(2,1)}, u32[]{:S(2)}) copy-start(bf16[1024,6,128]{2,0,1:T(8,128)(2,1)} %copy.116) | copy-start | bytes 4718596
  91.9 3.0 %copy-start.5 = (bf16[256,6,128]{2,0,1:T(8,128)(2,1)S(1)}, bf16[256,6,128]{2,0,1:T(8,128)(2,1)}, u32[]{:S(2)}) copy-start(bf16[256,6,128]{2,0,1:T(8,128)(2,1)} %copy.119) | copy-start | bytes 1179652
  91.9 3.0 %copy-start.8 = (bf16[128,6,128]{2,0,1:T(8,128)(2,1)S(1)}, bf16[128,6,128]{2,0,1:T(8,128)(2,1)}, u32[]{:S(2)}) copy-start(bf16[128,6,128]{2,0,1:T(8,128)(2,1)} %copy.118) | copy-start | bytes 589828
  94.8 35.4 %copy-start = (f32[6,1024,384]{1,2,0:T(8,128)}, f32[6,1024,384]{1,2,0:T(8,128)S(1)}, u32[]{:S(2)}) copy-start(f32[6,1024,384]{1,2,0:T(8,128)S(1)} %get-tuple-element.41) | copy-start | bytes 28311556
  94.8 35.4 %copy-start.6 = (f32[6,1024]{1,0:T(8,128)}, f32[6,1024]{1,0:T(8,128)S(1)}, u32[]{:S(2)}) copy-start(f32[6,1024]{1,0:T(8,128)S(1)} %get-tuple-element.40) | copy-start | bytes 73732
  130.2 3.5 %copy-start.12 = (f32[6,1024]{1,0:T(8,128)}, f32[6,1024]{1,0:T(8,128)S(1)}, u32[]{:S(2)}) copy-start(f32[6,1024]{1,0:T(8,128)S(1)} %get-tuple-element.38) | copy-start | bytes 73732
  130.3 5.7 %copy-start.4 = (bf16[128,6,128]{2,0,1:T(8,128)(2,1)S(1)}, bf16[128,6,128]{2,0,1:T(8,128)(2,1)}, u32[]{:S(2)}) copy-start(bf16[128,6,128]{2,0,1:T(8,128)(2,1)} %copy.109) | copy-start | bytes 589828
  133.7 2.2 %copy-start.1 = (bf16[6,1024,384]{1,2,0:T(8,128)(2,1)}, bf16[6,1024,384]{1,2,0:T(8,128)(2,1)S(1)}, u32[]{:S(2)}) copy-start(bf16[6,1024,384]{1,2,0:T(8,128)(2,1)S(1)} %multiply_convert_fusion) | copy-start | bytes 14155780
  140.7 9.2 %copy-start.7 = (f32[6,1024]{1,0:T(8,128)S(1)}, f32[6,1024]{1,0:T(8,128)}, u32[]{:S(2)}) copy-start(f32[6,1024]{1,0:T(8,128)} %copy-done.6) | copy-start | bytes 73732
  140.7 9.3 %copy-start.13 = (f32[6,1024]{1,0:T(8,128)S(1)}, f32[6,1024]{1,0:T(8,128)}, u32[]{:S(2)}) copy-start(f32[6,1024]{1,0:T(8,128)} %copy-done.12) | copy-start | bytes 73732
  144.6 0.8 copy-start.3
  146.6 10.2 %all-to-all-start.3 = ((bf16[4,32,768]{2,1,0:T(8,128)(2,1)}), bf16[4,32,768]{2,1,0:T(8,128)(2,1)S(1)}, u32[]{:S(2)}, u32[]{:S(2)}) async-start(bf16[4,32,768]{2,1,0:T(8,128)(2,1)} %all_to_all.74), calls=%async_computation.4 | async-start | bytes 393216 | tf_op jit(solution)/shard_map/all_to_all | solution.py:67
  149.9 57.6 %slice-start = ((bf16[384,6,128]{0,2,1:T(8,128)(2,1)}), bf16[256,6,128]{0,2,1:T(8,128)(2,1)S(1)}, s32[]{:S(2)}) async-start(bf16[384,6,128]{0,2,1:T(8,128)(2,1)} %copy-done.3), calls=%async_computation.8 | async-start | bytes 786432 | tf_op jit(solution)/shard_map/slice | solution.py:69
  204.2 8.7 %all-to-all-start.2 = ((bf16[4,32,768]{2,1,0:T(8,128)(2,1)}), bf16[4,32,768]{2,1,0:T(8,128)(2,1)S(1)}, u32[]{:S(2)}, u32[]{:S(2)}) async-start(bf16[4,32,768]{2,1,0:T(8,128)(2,1)} %bitcast.116), calls=%async_computation.3 | async-start | bytes 393216 | tf_op jit(solution)/shard_map/all_to_all | solution.py:67
Sparse Core Ops, SparseCore 0:
  22.2 60.7 all-gather.2
  140.8 63.3 reduce-scatter.1

commit v2 on v1

v2 whole, which is shorter than its diff:
```python
import functools
import math

import jax
import jax.numpy as jnp
from jax import lax
from jax.experimental import pallas as pl
from jax.experimental.pallas import tpu as pltpu
from jax.sharding import PartitionSpec as P

HS = 128
NZ = 4
SLOTS = 8
MESH = pl.DeviceIdType.MESH


def kernel(
    nt, nh,
    query, d_out, key_cur, value_cur, key_hist, value_hist, bias,
    out_q, out_k, out_v, out_kh, out_vh,
    qd, kv, dkv, dq, ry, rz, sz, st, st_in, fin, acc, fq, fkv,
    s_a, r_a, s_kv, r_kv, s_z, r_z, s_y, r_y, s_st, r_st, s_f, r_f,
    s_ry, r_ry, s_rz, r_rz, s_b, r_b, s_c, r_c,
):
    ny = nt // NZ
    rows = query.shape[0]
    feat = query.shape[1] // nh
    heads = feat // HS
    cur = rows * nh
    scale = 1.0 / math.sqrt(HS)
    scale2 = scale * math.log2(math.e)
    t, h = lax.axis_index("tm"), lax.axis_index("head")
    z, y = t // ny, t % ny

    def copy(src, dst, ss, rs, tm, hd):
        return pltpu.make_async_remote_copy(
            src_ref=src, dst_ref=dst, send_sem=ss, recv_sem=rs,
            device_id=(tm, hd), device_id_type=MESH,
        )

    barrier = pltpu.get_barrier_semaphore()
    for k in range(1, nt):
        pl.semaphore_signal(barrier, inc=1, device_id=((t + k) % nt, h), device_id_type=MESH)
    for k in range(1, nh):
        pl.semaphore_signal(barrier, inc=1, device_id=(t, (h + k) % nh), device_id_type=MESH)
    pl.semaphore_wait(barrier, nt + nh - 2)

    def cols(i):
        return pl.ds(pl.multiple_of(i * feat, HS), feat)

    def band(i):
        return pl.ds(pl.multiple_of(i * rows, rows), rows)

    def a_copy(k, i):
        src = (query, d_out)[i]
        p = (h + k) % nh
        return copy(src.at[:, cols(p)], qd.at[t, i, band(h), :], s_a.at[k - 1, i], r_a.at[k - 1, i], t, p)

    def kv_copy(k, i):
        src = (key_cur, value_cur)[i]
        p = (h + k) % nh
        return copy(src.at[:, cols(p)], kv.at[i, band(h), :], s_kv.at[k - 1, i], r_kv.at[k - 1, i], t, p)

    for start in (a_copy, kv_copy):
        for k in range(1, nh):
            for i in range(2):
                start(k, i).start()
    qd[t, 0, band(h), :] = query[:, cols(h)]
    qd[t, 1, band(h), :] = d_out[:, cols(h)]
    kv[0, band(h), :] = key_cur[:, cols(h)]
    kv[1, band(h), :] = value_cur[:, cols(h)]
    kv[0, cur:, :] = key_hist[...]
    kv[1, cur:, :] = value_hist[...]
    st[...] = jnp.zeros_like(st)
    dkv[...] = jnp.zeros_like(dkv)
    for k in range(1, nh):
        for i in range(2):
            a_copy(k, i).wait_recv()

    n_slot = 2 * NZ - 1

    def at_slot(slot):
        dist = (slot + 1) // 2
        up = slot % 2
        zz = jnp.where(up == 1, z - dist, z + dist)
        return zz, dist, up, (zz >= 0) & (zz < NZ)

    def z_copy(zz, way, hop):
        to = jnp.clip(z + (1 if way == 0 else -1), 0, NZ - 1)
        b = zz * ny + y
        return copy(qd.at[b], qd.at[b], s_z.at[way, hop], r_z.at[way, hop], to * ny + y, h)

    def y_copy(zz, slot, k):
        b = zz * ny + y
        return copy(qd.at[b], qd.at[b], s_y.at[slot, k - 1], r_y.at[slot, k - 1], z * ny + (y + k) % ny, h)

    def st_copy(b):
        return copy(st.at[b], st_in.at[t], s_st.at[b], r_st.at[t], b, h)

    def head_cols(i):
        return pl.ds(pl.multiple_of(i * HS, HS), HS)

    def nt_dot(a, b):
        return lax.dot_general(a, b, (((1,), (1,)), ((), ())), preferred_element_type=jnp.float32)

    def pass1(b):
        def one(i, c):
            hc = head_cols(i)
            s = nt_dot(kv[0, :, hc], qd[b, 0, :, hc]) * scale2 + bias[:, :cur]
            g = nt_dot(kv[1, :, hc], qd[b, 1, :, hc])
            m = jnp.max(s, axis=0, keepdims=True)
            w = jnp.exp2(s - m)
            st[b, 0, pl.ds(i, 1), :] = m
            st[b, 1, pl.ds(i, 1), :] = jnp.sum(w, axis=0, keepdims=True)
            st[b, 2, pl.ds(i, 1), :] = jnp.sum(w * g, axis=0, keepdims=True)
            return c

        lax.fori_loop(0, heads, one, 0)

        @pl.when(b != t)
        def _():
            st_copy(b).start()

    def gather_step(n, c):
        zz, dist, up, ok = at_slot(n)

        @pl.when((n < n_slot) & ok)
        def _():
            @pl.when(n == 0)
            def _():
                @pl.when(z + 1 < NZ)
                def _():
                    z_copy(zz, 0, 0).start()

                @pl.when(z > 0)
                def _():
                    z_copy(zz, 1, 0).start()

            for way in range(2):
                @pl.when((n > 0) & (up == 1 - way))
                def _():
                    z_copy(zz, way, dist - 1).wait_recv()

                    @pl.when((z + 1 < NZ) if way == 0 else (z > 0))
                    def _():
                        z_copy(zz, way, dist).start()

            for k in range(1, ny):
                y_copy(zz, n, k).start()

            @pl.when(n == 0)
            def _():
                for k in range(1, nh):
                    for i in range(2):
                        kv_copy(k, i).wait_recv()

            pass1(zz * ny + y)

        m = n - 2
        zm, _, _, okm = at_slot(jnp.maximum(m, 0))

        @pl.when((m >= 0) & okm)
        def _():
            def from_peer(k, cc):
                y_copy(zm, m, k).wait_recv()
                pass1(zm * ny + (y + ny - k) % ny)
                return cc

            lax.fori_loop(1, ny, from_peer, 0)

        return c

    lax.fori_loop(0, n_slot + 2, gather_step, 0)

    st_in[t] = st[t]
    for k in range(1, nt):
        src = (t + nt - k) % nt
        copy(st.at[t], st_in.at[src], s_st.at[src], r_st.at[src], src, h).wait_recv()
    top = jnp.max(st_in[:, 0], axis=0)
    back = jnp.exp2(st_in[:, 0] - top[None])
    total = jnp.sum(st_in[:, 1] * back, axis=0)
    total = jnp.where(total > 0, total, 1.0)
    fin[t, 0] = top
    fin[t, 1] = 1.0 / total
    fin[t, 2] = jnp.sum(st_in[:, 2] * back, axis=0) / total

    def f_copy(k):
        return copy(fin.at[t], fin.at[t], s_f.at[k - 1], r_f.at[k - 1], (t + k) % nt, h)

    for k in range(1, nt):
        f_copy(k).start()
    for k in range(1, nt):
        f_copy(k).wait_recv()

    tile = 2 * cur

    def order(i):
        return jnp.where(z < NZ // 2, NZ - 1 - i, i)

    def ry_copy(d, k):
        p = (y + k) % ny
        return copy(dq.at[d * ny + p], ry.at[d, k - 1], s_ry.at[d, k - 1], r_ry.at[d, k - 1], z * ny + p, h)

    def pass2(n, c):
        d = order(n)

        def pair(j, cc):
            b = d * ny + 2 * j

            def one(i, ccc):
                hc = head_cols(i)
                key, val = kv[0, :, hc], kv[1, :, hc]
                q = jnp.concatenate([qd[b, 0, :, hc], qd[b + 1, 0, :, hc]], axis=0)
                do = jnp.concatenate([qd[b, 1, :, hc], qd[b + 1, 1, :, hc]], axis=0)

                def stat(r):
                    return jnp.concatenate([fin[b, r, pl.ds(i, 1), :], fin[b + 1, r, pl.ds(i, 1), :]], axis=1)

                s = nt_dot(key, q) * scale2 + bias[...]
                g = nt_dot(val, do)
                p = jnp.exp2(s - stat(0)) * stat(1)
                sg = (p * scale * (g - stat(2))).astype(jnp.bfloat16)
                dkv[0, :, hc] += jnp.dot(sg, q, preferred_element_type=jnp.float32)
                dkv[1, :, hc] += jnp.dot(p.astype(jnp.bfloat16), do, preferred_element_type=jnp.float32)
                part = lax.dot_general(
                    sg, key, (((0,), (0,)), ((), ())), preferred_element_type=jnp.float32
                ).astype(jnp.bfloat16)
                dq[b, :, hc] = part[:cur]
                dq[b + 1, :, hc] = part[cur:]
                return ccc

            lax.fori_loop(0, heads, one, 0)
            return cc

        lax.fori_loop(0, ny // 2, pair, 0)
        for k in range(1, ny):
            ry_copy(d, k).start()
        return c

    lax.fori_loop(0, NZ, pass2, 0)

    def b_copy(k, i):
        p = (h + k) % nh
        dst = (out_k, out_v)[i]
        return copy(fkv.at[i, band(p), :], dst.at[:, cols(h)], s_b.at[k - 1, i], r_b.at[k - 1, i], t, p)

    fkv[...] = dkv[:, :cur, :].astype(jnp.bfloat16)
    for k in range(1, nh):
        for i in range(2):
            b_copy(k, i).start()
    out_k[:, cols(h)] = fkv[0, band(h), :]
    out_v[:, cols(h)] = fkv[1, band(h), :]
    out_kh[...] = dkv[0, cur:, :].astype(jnp.bfloat16)
    out_vh[...] = dkv[1, cur:, :].astype(jnp.bfloat16)

    def rz_copy(d, way):
        to = jnp.clip(z + (1 if way == 0 else -1), 0, NZ - 1)
        return copy(sz.at[d], rz.at[way, d], s_rz.at[way, d], r_rz.at[way, d], to * ny + y, h)

    def own_sum(d):
        acc[...] = dq[d * ny + y].astype(jnp.float32)
        for k in range(1, ny):
            ry_copy(d, k).wait_recv()
            acc[...] += ry[d, k - 1].astype(jnp.float32)

        @pl.when((z <= d) & (z > 0))
        def _():
            rz_copy(d, 0).wait_recv()
            acc[...] += rz[0, d].astype(jnp.float32)

        @pl.when((z >= d) & (z < NZ - 1))
        def _():
            rz_copy(d, 1).wait_recv()
            acc[...] += rz[1, d].astype(jnp.float32)

    def chain(n, c):
        d = order(n)

        @pl.when(d != z)
        def _():
            own_sum(d)
            sz[d] = acc[...].astype(jnp.bfloat16)

            @pl.when(z < d)
            def _():
                rz_copy(d, 0).start()

            @pl.when(z > d)
            def _():
                rz_copy(d, 1).start()

        return c

    lax.fori_loop(0, NZ, chain, 0)
    own_sum(z)
    fq[...] = acc[...].astype(jnp.bfloat16)

    def c_copy(k):
        p = (h + k) % nh
        return copy(fq.at[band(p), :], out_q.at[:, cols(h)], s_c.at[k - 1], r_c.at[k - 1], t, p)

    for k in range(1, nh):
        c_copy(k).start()
    out_q[:, cols(h)] = fq[band(h), :]

    for k in range(1, nh):
        c_copy(k).wait()
        for i in range(2):
            b_copy(k, i).wait()
            a_copy(k, i).wait_send()
            kv_copy(k, i).wait_send()
    for k in range(1, nt):
        f_copy(k).wait_send()
        st_copy((t + k) % nt).wait_send()

    def sent(n, c):
        zz, dist, up, ok = at_slot(n)

        @pl.when(ok)
        def _():
            for k in range(1, ny):
                y_copy(zz, n, k).wait_send()
            for way in range(2):
                @pl.when(((n == 0) | (up == 1 - way)) & ((z + 1 < NZ) if way == 0 else (z > 0)))
                def _():
                    z_copy(zz, way, dist).wait_send()

        return c

    lax.fori_loop(0, n_slot, sent, 0)

    def reduced(d, c):
        for k in range(1, ny):
            ry_copy(d, k).wait_send()

        @pl.when(z < d)
        def _():
            rz_copy(d, 0).wait_send()

        @pl.when(z > d)
        def _():
            rz_copy(d, 1).wait_send()

        return c

    lax.fori_loop(0, NZ, reduced, 0)


def shards(query, key_cur, value_cur, d_out, key_hist, value_hist, hist_len):
    nt, nh = lax.axis_size("tm"), lax.axis_size("head")
    ny = nt // NZ
    rows, width = query.shape
    feat = width // nh
    cur = rows * nh
    n_k = cur + key_hist.shape[0]
    slot = jnp.arange(n_k)
    live = (slot < cur) | (slot - cur < hist_len[0])
    bias = jnp.broadcast_to(jnp.where(live, 0.0, -1e30).astype(jnp.float32)[:, None], (n_k, 2 * cur))
    bf, f32 = jnp.bfloat16, jnp.float32
    vmem = pl.BlockSpec(memory_space=pltpu.VMEM)

    def sems(*dims):
        return pltpu.SemaphoreType.DMA(dims)

    out = jax.ShapeDtypeStruct
    return pl.pallas_call(
        functools.partial(kernel, nt, nh),
        out_shape=(
            out((rows, width), bf), out((rows, width), bf), out((rows, width), bf),
            out(key_hist.shape, bf), out(value_hist.shape, bf),
        ),
        in_specs=[vmem] * 7,
        out_specs=(vmem,) * 5,
        scratch_shapes=[
            pltpu.VMEM((nt, 2, cur, feat), bf),
            pltpu.VMEM((2, n_k, feat), bf),
            pltpu.VMEM((2, n_k, feat), f32),
            pltpu.VMEM((nt, cur, feat), bf),
            pltpu.VMEM((NZ, ny - 1, cur, feat), bf),
            pltpu.VMEM((2, NZ, cur, feat), bf),
            pltpu.VMEM((NZ, cur, feat), bf),
            pltpu.VMEM((nt, 3, SLOTS, cur), f32),
            pltpu.VMEM((nt, 3, SLOTS, cur), f32),
            pltpu.VMEM((nt, 3, SLOTS, cur), f32),
            pltpu.VMEM((cur, feat), f32),
            pltpu.VMEM((cur, feat), bf),
            pltpu.VMEM((2, cur, feat), bf),
            sems(nh - 1, 2), sems(nh - 1, 2), sems(nh - 1, 2), sems(nh - 1, 2),
            sems(2, NZ), sems(2, NZ), sems(2 * NZ - 1, ny - 1), sems(2 * NZ - 1, ny - 1),
            sems(nt), sems(nt), sems(nt - 1), sems(nt - 1),
            sems(NZ, ny - 1), sems(NZ, ny - 1), sems(2, NZ), sems(2, NZ),
            sems(nh - 1, 2), sems(nh - 1, 2), sems(nh - 1), sems(nh - 1),
        ],
        compiler_params=pltpu.CompilerParams(
            collective_id=0, has_side_effects=True, vmem_limit_bytes=52 * 1024 * 1024
        ),
        name="attention_backward",
    )(query, d_out, key_cur, value_cur, key_hist, value_hist, bias)


def solution(mesh):
    tok, hist = P(("tm", "head"), None), P("tm", "head")
    return jax.shard_map(
        shards,
        mesh=mesh,
        in_specs=(tok, tok, tok, tok, hist, hist, P("tm")),
        out_specs=(tok, tok, tok, hist, hist),
        check_vma=False,
    )
```

time: 221 us -> 107 us (0.48)
  Pallas kernels: 0 us -> 98.9 us
  waiting for transfers between devices: 92.1 us -> 0 us
  blocking collectives: 52.2 us -> 0 us
  local copies, waits for them, and re-layouts: 28.5 us -> 6.85 us
  matrix products: 18.1 us -> 0 us
  between operations: 15.1 us -> 1.32 us
  starting transfers between devices: 10.3 us -> 0 us
  other arithmetic: 4.1 us -> 0.01 us
    pallas_call x0 -> x1, Pallas kernels: none -> 98.9 us  [shards(): pl.pallas_call(functools.partial(kernel, nt, nh), out_shape=(out((rows, w...]
    all_gather x1 -> x0, waiting for transfers between devices: 45.9 us -> none  [shards(): both = lax.all_gather(both, 'tm', axis=1, tiled=True)]
    reduce_scatter x1 -> x0, waiting for transfers between devices: 39 us -> none  [shards(): gq = lax.psum_scatter(gq, 'tm', scatter_dimension=0, tiled=True)]
    all_gather x1 -> x0, blocking collectives: 32.3 us -> none  [shards(): lax.all_gather(jnp.stack([m, total, dots]), 'tm', axis=0, tiled=False)]
    all_to_all x2 -> x0, blocking collectives: 19.8 us -> none  [the longest x1 11.5 us: shards(): both = lax.all_to_all(both, 'head', split_axis=2, concat_axis=1, tiled=True)]
    dot_general x5 -> x0, matrix products: 18.1 us -> none  [the longest x1 6.31 us: shards(): jnp.einsum('hqk,hqd->khd', prob, gh, preferred_element_type=jnp.float32)]
    all_to_all x3 -> x0, starting transfers between devices: 10.2 us -> none  [the longest x2 6.73 us: to_tokens(): return lax.all_to_all(x, 'head', split_axis=0, concat_axis=1, tiled=True)]
    another operation x8 -> x0, local copies, waits for them, and re-layouts: 7.4 us -> none  [the longest x2 3.17 us: by_head(): return x.reshape(x.shape[0], heads, HS).transpose(1, 0, 2)]
  transfers between devices with their start and end apart: 5 -> 0, of which waited for: 4 -> 0; matrix products, arithmetic and copies ran while one was open for 9% -> 0% of each run, Pallas kernels for 0% -> 0%
where the time goes in v2:
time: 107 us
  Pallas kernels  98.9 us (92%)
  local copies, waits for them, and re-layouts  6.85 us (6%)
  between operations  1.32 us (1%)
    pallas_call x1, Pallas kernels, shards(): pl.pallas_call(functools.partial(kernel, nt, nh), out_shape=(out((rows, w...  98.9 us
    unnamed x15, local copies, waits for them, and re-layouts  5.98 us

profile of v2, /device:TPU:0, one launch (start us, length us, event | category | flops | bytes accessed | tf_op | source)
XLA Modules:
  0.0 107.1 jit_solution(985008824720283085)
XLA Ops:
  1.3 0.0 copy-start
  1.3 0.0 copy-start.1
  1.3 0.9 broadcast_in_dim.16.bias
  2.2 0.0 copy-done
  2.2 0.2 copy-done.1
  2.4 0.0 copy-start.2
  2.4 0.9 copy-done.2
  3.3 0.0 copy-start.3
  3.3 0.9 copy-done.3
  4.2 98.9 %attention_backward.1 = (bf16[32,3072]{1,0:T(8,128)(2,1)S(1)}, bf16[32,3072]{1,0:T(8,128)(2,1)S(1)}, bf16[32,3072]{1,0:T(8,128)(2,1)S(1)}, bf16[256,768]{1,0:T(8,128)(2,1)S(1)}, bf16[256,768]{1,0:T(8,128)(2,1)}) custom-call(bf16[32,3072]{1,0:T(8,128)(2,1)S(1)} %copy-done, bf16[32,3072]{1,0:T(8,128)(2,1)S(1)} %copy-done.1, bf16[32,3072]{1,0:T(8,128)(2,1)S(1)} %copy-done.2, ...), custom_call_target="tpu_custom_call" | custom-call | tf_op jit(solution)/shard_map/attention_backward/pallas_call | solution.py:366
  103.2 0.7 copy.18
  103.9 0.7 copy.19
  104.5 0.7 copy.20
  105.2 0.0 copy-start.4
  105.2 0.7 copy.21
  106.0 0.4 copy-done.4
  106.4 0.7 copy.22
  (1 shorter events, 0.0 us)
Async XLA Ops:
  1.3 0.9 copy-start
  1.3 1.1 %copy-start.1 = (bf16[32,3072]{1,0:T(8,128)(2,1)S(1)}, bf16[32,3072]{1,0:T(8,128)(2,1)}, u32[]{:S(2)}) copy-start(bf16[32,3072]{1,0:T(8,128)(2,1)} %d_out.1) | copy-start | bytes 589828
  2.4 0.9 copy-start.2
  3.3 0.9 copy-start.3
  105.2 1.1 %copy-start.4 = (bf16[256,768]{1,0:T(8,128)(2,1)S(1)}, bf16[256,768]{1,0:T(8,128)(2,1)}, u32[]{:S(2)}) copy-start(bf16[256,768]{1,0:T(8,128)(2,1)} %get-tuple-element.14) | copy-start | bytes 1179652

commit v3 on v1

v3 whole, which is shorter than its diff:
```python
import functools
import math

import jax
import jax.numpy as jnp
from jax import lax
from jax.experimental import pallas as pl
from jax.experimental.pallas import tpu as pltpu
from jax.sharding import PartitionSpec as P

HS = 128
NZ = 4
SLOTS = 8
MESH = pl.DeviceIdType.MESH


def kernel(
    nt, nh, nc,
    hist_len, query, d_out, key_cur, value_cur, key_hist, value_hist,
    out_q, out_k, out_v, out_kh, out_vh,
    qd, kv, dkv, dq, ry, rz, sz, st, st_in, fin, acc, fq, fkv, bias,
    s_a, r_a, s_kv, r_kv, s_z, r_z, s_y, r_y, s_st, r_st, s_f, r_f,
    s_ry, r_ry, s_rz, r_rz, s_b, r_b, s_c, r_c, s_own, s_hist, s_oc,
):
    ny = nt // NZ
    rows = query.shape[0]
    feat = query.shape[1] // nh
    heads = feat // HS
    hpc = heads // nc
    width = hpc * HS
    cur = rows * nh
    n_k = kv.shape[1]
    scale = 1.0 / math.sqrt(HS)
    scale2 = scale * math.log2(math.e)
    t, h = lax.axis_index("tm"), lax.axis_index("head")
    z, y = t // ny, t % ny

    def copy(src, dst, ss, rs, tm, hd):
        return pltpu.make_async_remote_copy(
            src_ref=src, dst_ref=dst, send_sem=ss, recv_sem=rs,
            device_id=(tm, hd), device_id_type=MESH,
        )

    def cols(i, c):
        return pl.ds(pl.multiple_of(i * feat + c * width, HS), width)

    def part(c):
        return pl.ds(pl.multiple_of(c * width, HS), width)

    def band(i):
        return pl.ds(pl.multiple_of(i * rows, rows), rows)

    def own_copy(c, i):
        src = (query, d_out)[i]
        return pltpu.make_async_copy(src.at[:, cols(h, c)], qd.at[c, t, i, band(h), :], s_own.at[c, i])

    def own_kv(i):
        src = (key_cur, value_cur)[i]
        return pltpu.make_async_copy(
            src.at[:, pl.ds(pl.multiple_of(h * feat, HS), feat)], kv.at[i, band(h), :], s_oc.at[i]
        )

    def hist_copy(i):
        return pltpu.make_async_copy((key_hist, value_hist)[i], kv.at[i, pl.ds(cur, n_k - cur), :], s_hist.at[i])

    def a_copy(c, k, i):
        src = (query, d_out)[i]
        p = (h + k) % nh
        return copy(
            src.at[:, cols(p, c)], qd.at[c, t, i, band(h), :], s_a.at[c, k - 1, i], r_a.at[c, k - 1, i], t, p
        )

    def kv_copy(c, k, i):
        src = (key_cur, value_cur)[i]
        p = (h + k) % nh
        return copy(
            src.at[:, cols(p, c)], kv.at[i, band(h), part(c)], s_kv.at[c, k - 1, i], r_kv.at[c, k - 1, i], t, p
        )

    for i in range(2):
        for c in range(nc):
            own_copy(c, i).start()
        own_kv(i).start()
        hist_copy(i).start()

    barrier = pltpu.get_barrier_semaphore()
    for k in range(1, nt):
        pl.semaphore_signal(barrier, inc=1, device_id=((t + k) % nt, h), device_id_type=MESH)
    for k in range(1, nh):
        pl.semaphore_signal(barrier, inc=1, device_id=(t, (h + k) % nh), device_id_type=MESH)
    pl.semaphore_wait(barrier, nt + nh - 2)

    def exchange(c, cc):
        for start in (a_copy, kv_copy):
            for k in range(1, nh):
                for i in range(2):
                    start(c, k, i).start()
        return cc

    lax.fori_loop(0, nc, exchange, 0)
    st[...] = jnp.zeros_like(st)
    dkv[...] = jnp.zeros_like(dkv)
    slot_row = lax.broadcasted_iota(jnp.int32, bias.shape, 0)
    bias[...] = jnp.where(slot_row < cur + hist_len[0], 0.0, -1e30)
    for i in range(2):
        own_kv(i).wait()
        hist_copy(i).wait()

    n_slot = 2 * NZ - 1

    def at_slot(slot):
        dist = (slot + 1) // 2
        up = slot % 2
        zz = jnp.where(up == 1, z - dist, z + dist)
        return zz, dist, up, (zz >= 0) & (zz < NZ)

    def z_copy(c, zz, way, hop):
        to = jnp.clip(z + (1 if way == 0 else -1), 0, NZ - 1)
        b = zz * ny + y
        return copy(qd.at[c, b], qd.at[c, b], s_z.at[c, way, hop], r_z.at[c, way, hop], to * ny + y, h)

    def y_copy(c, zz, slot, k):
        b = zz * ny + y
        p = z * ny + (y + k) % ny
        return copy(qd.at[c, b], qd.at[c, b], s_y.at[c, slot, k - 1], r_y.at[c, slot, k - 1], p, h)

    def st_copy(c, b):
        return copy(st.at[c, b], st_in.at[c, t], s_st.at[c, b], r_st.at[c, t], b, h)

    def head_cols(i):
        return pl.ds(pl.multiple_of(i * HS, HS), HS)

    def nt_dot(a, b):
        return lax.dot_general(a, b, (((1,), (1,)), ((), ())), preferred_element_type=jnp.float32)

    def pass1(c, b):
        for i in range(hpc):
            hc, lc = head_cols(c * hpc + i), slice(i * HS, (i + 1) * HS)
            s = nt_dot(kv[0, :, hc], qd[c, b, 0, :, lc]) * scale2 + bias[:, :cur]
            g = nt_dot(kv[1, :, hc], qd[c, b, 1, :, lc])
            m = jnp.max(s, axis=0, keepdims=True)
            w = jnp.exp2(s - m)
            st[c, b, i : i + 1, :] = m
            st[c, b, hpc + i : hpc + i + 1, :] = jnp.sum(w, axis=0, keepdims=True)
            st[c, b, 2 * hpc + i : 2 * hpc + i + 1, :] = jnp.sum(w * g, axis=0, keepdims=True)

        @pl.when(b != t)
        def _():
            st_copy(c, b).start()

    def own_sends(c):
        for i in range(2):
            own_copy(c, i).wait()
            for k in range(1, nh):
                a_copy(c, k, i).wait_recv()

        @pl.when(z + 1 < NZ)
        def _():
            z_copy(c, z, 0, 0).start()

        @pl.when(z > 0)
        def _():
            z_copy(c, z, 1, 0).start()

        for k in range(1, ny):
            y_copy(c, z, 0, k).start()

    def gather_step(n, c):
        zz, dist, up, ok = at_slot(n)

        @pl.when((n < n_slot) & ok)
        def _():
            for way in range(2):
                @pl.when((n > 0) & (up == 1 - way))
                def _():
                    z_copy(c, zz, way, dist - 1).wait_recv()

                    @pl.when((z + 1 < NZ) if way == 0 else (z > 0))
                    def _():
                        z_copy(c, zz, way, dist).start()

            @pl.when(n > 0)
            def _():
                for k in range(1, ny):
                    y_copy(c, zz, n, k).start()

            @pl.when(n == 0)
            def _():
                for k in range(1, nh):
                    for i in range(2):
                        kv_copy(c, k, i).wait_recv()

            pass1(c, zz * ny + y)

        m = n - 2
        zm, _, _, okm = at_slot(jnp.maximum(m, 0))

        @pl.when((m >= 0) & okm)
        def _():
            def from_peer(k, cc):
                y_copy(c, zm, m, k).wait_recv()
                pass1(c, zm * ny + (y + ny - k) % ny)
                return cc

            lax.fori_loop(1, ny, from_peer, 0)

        return c

    def f_copy(c, k):
        return copy(fin.at[c, t], fin.at[c, t], s_f.at[c, k - 1], r_f.at[c, k - 1], (t + k) % nt, h)

    def join(c):
        st_in[c, t] = st[c, t]
        for k in range(1, nt):
            src = (t + nt - k) % nt
            copy(st.at[c, t], st_in.at[c, src], s_st.at[c, src], r_st.at[c, src], src, h).wait_recv()
        local = st_in[c]
        top = jnp.max(local[:, :hpc], axis=0)
        back = jnp.exp2(local[:, :hpc] - top[None])
        total = jnp.sum(local[:, hpc : 2 * hpc] * back, axis=0)
        dots = jnp.sum(local[:, 2 * hpc : 3 * hpc] * back, axis=0)
        fin[c, t] = jnp.zeros_like(fin[c, t])
        fin[c, t, :hpc, :] = top
        fin[c, t, hpc : 2 * hpc, :] = 1.0 / total
        fin[c, t, 2 * hpc : 3 * hpc, :] = dots / total
        for k in range(1, nt):
            f_copy(c, k).start()

    def order(i):
        return jnp.where(z < NZ // 2, NZ - 1 - i, i)

    def ry_copy(c, d, k):
        p = (y + k) % ny
        return copy(
            dq.at[c, d * ny + p], ry.at[c, d, k - 1], s_ry.at[c, d, k - 1], r_ry.at[c, d, k - 1], z * ny + p, h
        )

    def b_copy(c, k, i):
        p = (h + k) % nh
        dst = (out_k, out_v)[i]
        return copy(
            fkv.at[i, band(p), part(c)], dst.at[:, cols(h, c)], s_b.at[c, k - 1, i], r_b.at[c, k - 1, i], t, p
        )

    def pass2(c):
        for k in range(1, nt):
            f_copy(c, k).wait_recv()

        def group(n, cc):
            d = order(n)

            def pair(j, ccc):
                b = d * ny + 2 * j
                for i in range(hpc):
                    hc, lc = head_cols(c * hpc + i), slice(i * HS, (i + 1) * HS)
                    key, val = kv[0, :, hc], kv[1, :, hc]
                    q = jnp.concatenate([qd[c, b, 0, :, lc], qd[c, b + 1, 0, :, lc]], axis=0)
                    do = jnp.concatenate([qd[c, b, 1, :, lc], qd[c, b + 1, 1, :, lc]], axis=0)

                    def stat(r):
                        row = r * hpc + i
                        return jnp.concatenate(
                            [fin[c, b, row : row + 1, :], fin[c, b + 1, row : row + 1, :]], axis=1
                        )

                    s = nt_dot(key, q) * scale2 + bias[...]
                    g = nt_dot(val, do)
                    p = jnp.exp2(s - stat(0)) * stat(1)
                    sg = (p * scale * (g - stat(2))).astype(jnp.bfloat16)
                    dkv[0, :, hc] += jnp.dot(sg, q, preferred_element_type=jnp.float32)
                    dkv[1, :, hc] += jnp.dot(p.astype(jnp.bfloat16), do, preferred_element_type=jnp.float32)
                    term = lax.dot_general(
                        sg, key, (((0,), (0,)), ((), ())), preferred_element_type=jnp.float32
                    ).astype(jnp.bfloat16)
                    dq[c, b, :, lc] = term[:cur]
                    dq[c, b + 1, :, lc] = term[cur:]
                return ccc

            lax.fori_loop(0, ny // 2, pair, 0)
            for k in range(1, ny):
                ry_copy(c, d, k).start()
            return cc

        lax.fori_loop(0, NZ, group, 0)
        for i in range(2):
            fkv[i, :, part(c)] = dkv[i, :cur, part(c)].astype(jnp.bfloat16)
            for k in range(1, nh):
                b_copy(c, k, i).start()
            out = (out_k, out_v)[i]
            out[:, cols(h, c)] = fkv[i, band(h), part(c)]
            out = (out_kh, out_vh)[i]
            out[:, part(c)] = dkv[i, cur:, part(c)].astype(jnp.bfloat16)

    def rz_copy(c, d, way):
        to = jnp.clip(z + (1 if way == 0 else -1), 0, NZ - 1)
        return copy(sz.at[c, d], rz.at[c, way, d], s_rz.at[c, way, d], r_rz.at[c, way, d], to * ny + y, h)

    def own_sum(c, d):
        acc[...] = dq[c, d * ny + y].astype(jnp.float32)
        for k in range(1, ny):
            ry_copy(c, d, k).wait_recv()
            acc[...] += ry[c, d, k - 1].astype(jnp.float32)

        @pl.when((z <= d) & (z > 0))
        def _():
            rz_copy(c, d, 0).wait_recv()
            acc[...] += rz[c, 0, d].astype(jnp.float32)

        @pl.when((z >= d) & (z < NZ - 1))
        def _():
            rz_copy(c, d, 1).wait_recv()
            acc[...] += rz[c, 1, d].astype(jnp.float32)

    def c_copy(c, k):
        p = (h + k) % nh
        return copy(fq.at[c, band(p), :], out_q.at[:, cols(h, c)], s_c.at[c, k - 1], r_c.at[c, k - 1], t, p)

    def reduce_query(c):
        def chain(n, cc):
            d = order(n)

            @pl.when(d != z)
            def _():
                own_sum(c, d)
                sz[c, d] = acc[...].astype(jnp.bfloat16)

                @pl.when(z < d)
                def _():
                    rz_copy(c, d, 0).start()

                @pl.when(z > d)
                def _():
                    rz_copy(c, d, 1).start()

            return cc

        lax.fori_loop(0, NZ, chain, 0)
        own_sum(c, z)
        fq[c] = acc[...].astype(jnp.bfloat16)
        for k in range(1, nh):
            c_copy(c, k).start()
        out_q[:, cols(h, c)] = fq[c, band(h), :]

    own_sends(0)

    def stage(c, cc):
        @pl.when(c < nc)
        def _():
            lax.fori_loop(0, n_slot + 2, gather_step, c)

        @pl.when(c + 1 < nc)
        def _():
            own_sends(c + 1)

        @pl.when((c >= 1) & (c <= nc))
        def _():
            pass2(c - 1)

        @pl.when(c < nc)
        def _():
            join(c)

        @pl.when(c >= 2)
        def _():
            reduce_query(c - 2)

        return cc

    lax.fori_loop(0, nc + 2, stage, 0)

    def finish(c, cc):
        for k in range(1, nh):
            c_copy(c, k).wait()
            for i in range(2):
                b_copy(c, k, i).wait()
                a_copy(c, k, i).wait_send()
                kv_copy(c, k, i).wait_send()
        for k in range(1, nt):
            f_copy(c, k).wait_send()
            st_copy(c, (t + k) % nt).wait_send()

        def sent(n, ccc):
            zz, dist, up, ok = at_slot(n)

            @pl.when(ok)
            def _():
                for k in range(1, ny):
                    y_copy(c, zz, n, k).wait_send()
                for way in range(2):
                    @pl.when(((n == 0) | (up == 1 - way)) & ((z + 1 < NZ) if way == 0 else (z > 0)))
                    def _():
                        z_copy(c, zz, way, dist).wait_send()

            return ccc

        lax.fori_loop(0, n_slot, sent, 0)

        def reduced(d, ccc):
            for k in range(1, ny):
                ry_copy(c, d, k).wait_send()

            @pl.when(z < d)
            def _():
                rz_copy(c, d, 0).wait_send()

            @pl.when(z > d)
            def _():
                rz_copy(c, d, 1).wait_send()

            return ccc

        lax.fori_loop(0, NZ, reduced, 0)
        return cc

    lax.fori_loop(0, nc, finish, 0)


def shards(query, key_cur, value_cur, d_out, key_hist, value_hist, hist_len):
    nt, nh = lax.axis_size("tm"), lax.axis_size("head")
    ny = nt // NZ
    rows, width = query.shape
    feat = width // nh
    cur = rows * nh
    n_k = cur + key_hist.shape[0]
    nc = 3 if feat % (3 * HS) == 0 else 1
    wide = feat // nc
    hbm = pl.BlockSpec(memory_space=pl.ANY)
    bf, f32 = jnp.bfloat16, jnp.float32
    vmem = pl.BlockSpec(memory_space=pltpu.VMEM)

    def sems(*dims):
        return pltpu.SemaphoreType.DMA(dims)

    out = jax.ShapeDtypeStruct
    return pl.pallas_call(
        functools.partial(kernel, nt, nh, nc),
        out_shape=(
            out((rows, width), bf), out((rows, width), bf), out((rows, width), bf),
            out(key_hist.shape, bf), out(value_hist.shape, bf),
        ),
        in_specs=[pl.BlockSpec(memory_space=pltpu.SMEM)] + [hbm] * 6,
        out_specs=(vmem,) * 5,
        scratch_shapes=[
            pltpu.VMEM((nc, nt, 2, cur, wide), bf),
            pltpu.VMEM((2, n_k, feat), bf),
            pltpu.VMEM((2, n_k, feat), f32),
            pltpu.VMEM((nc, nt, cur, wide), bf),
            pltpu.VMEM((nc, NZ, ny - 1, cur, wide), bf),
            pltpu.VMEM((nc, 2, NZ, cur, wide), bf),
            pltpu.VMEM((nc, NZ, cur, wide), bf),
            pltpu.VMEM((nc, nt, SLOTS, cur), f32),
            pltpu.VMEM((nc, nt, SLOTS, cur), f32),
            pltpu.VMEM((nc, nt, SLOTS, cur), f32),
            pltpu.VMEM((cur, wide), f32),
            pltpu.VMEM((nc, cur, wide), bf),
            pltpu.VMEM((2, cur, feat), bf),
            pltpu.VMEM((n_k, 2 * cur), f32),
            sems(nc, nh - 1, 2), sems(nc, nh - 1, 2), sems(nc, nh - 1, 2), sems(nc, nh - 1, 2),
            sems(nc, 2, NZ), sems(nc, 2, NZ), sems(nc, 2 * NZ - 1, ny - 1), sems(nc, 2 * NZ - 1, ny - 1),
            sems(nc, nt), sems(nc, nt), sems(nc, nt - 1), sems(nc, nt - 1),
            sems(nc, NZ, ny - 1), sems(nc, NZ, ny - 1), sems(nc, 2, NZ), sems(nc, 2, NZ),
            sems(nc, nh - 1, 2), sems(nc, nh - 1, 2), sems(nc, nh - 1), sems(nc, nh - 1),
            sems(nc, 2), sems(2), sems(2),
        ],
        compiler_params=pltpu.CompilerParams(
            collective_id=0, has_side_effects=True, vmem_limit_bytes=52 * 1024 * 1024
        ),
        name="attention_backward",
    )(hist_len, query, d_out, key_cur, value_cur, key_hist, value_hist)


def solution(mesh):
    tok, hist = P(("tm", "head"), None), P("tm", "head")
    return jax.shard_map(
        shards,
        mesh=mesh,
        in_specs=(tok, tok, tok, tok, hist, hist, P("tm")),
        out_specs=(tok, tok, tok, hist, hist),
        check_vma=False,
    )
```

time: 221 us -> 121 us (0.55)
  Pallas kernels: 0 us -> 111 us
  waiting for transfers between devices: 92.1 us -> 0 us
  blocking collectives: 52.2 us -> 0 us
  local copies, waits for them, and re-layouts: 28.5 us -> 7.61 us
  matrix products: 18.1 us -> 0 us
  between operations: 15.1 us -> 1.3 us
  starting transfers between devices: 10.3 us -> 0 us
  other arithmetic: 4.1 us -> 0 us
    pallas_call x0 -> x1, Pallas kernels: none -> 111 us  [shards(): pl.pallas_call(functools.partial(kernel, nt, nh, nc), out_shape=(out((row...]
    all_gather x1 -> x0, waiting for transfers between devices: 45.9 us -> none  [shards(): both = lax.all_gather(both, 'tm', axis=1, tiled=True)]
    reduce_scatter x1 -> x0, waiting for transfers between devices: 39 us -> none  [shards(): gq = lax.psum_scatter(gq, 'tm', scatter_dimension=0, tiled=True)]
    all_gather x1 -> x0, blocking collectives: 32.3 us -> none  [shards(): lax.all_gather(jnp.stack([m, total, dots]), 'tm', axis=0, tiled=False)]
    all_to_all x2 -> x0, blocking collectives: 19.8 us -> none  [the longest x1 11.5 us: shards(): both = lax.all_to_all(both, 'head', split_axis=2, concat_axis=1, tiled=True)]
    dot_general x5 -> x0, matrix products: 18.1 us -> none  [the longest x1 6.31 us: shards(): jnp.einsum('hqk,hqd->khd', prob, gh, preferred_element_type=jnp.float32)]
    all_to_all x3 -> x0, starting transfers between devices: 10.2 us -> none  [the longest x2 6.73 us: to_tokens(): return lax.all_to_all(x, 'head', split_axis=0, concat_axis=1, tiled=True)]
    another operation x8 -> x0, local copies, waits for them, and re-layouts: 7.4 us -> none  [the longest x2 3.17 us: by_head(): return x.reshape(x.shape[0], heads, HS).transpose(1, 0, 2)]
  transfers between devices with their start and end apart: 5 -> 0, of which waited for: 4 -> 0; matrix products, arithmetic and copies ran while one was open for 9% -> 0% of each run, Pallas kernels for 0% -> 0%
where the time goes in v3:
time: 121 us; the launch traced here: 120 us
  Pallas kernels  111 us (92%)
  local copies, waits for them, and re-layouts  7.61 us (6%)
  between operations  1.3 us (1%)
    pallas_call x1, Pallas kernels, shards(): pl.pallas_call(functools.partial(kernel, nt, nh, nc), out_shape=(out((row...  111 us
    unnamed x15, local copies, waits for them, and re-layouts  7.61 us

profile of v3, /device:TPU:0, one launch (start us, length us, event | category | flops | bytes accessed | tf_op | source)
XLA Modules:
  0.0 120.3 jit_solution(12339342785194823171)
XLA Ops:
  1.3 0.0 copy-start
  1.3 0.9 copy-done
  2.2 0.0 copy-start.1
  2.2 0.9 copy-done.1
  3.1 0.0 copy-start.2
  3.1 0.9 copy-done.2
  4.1 0.0 copy-start.3
  4.1 0.9 copy-done.3
  5.0 111.3 %attention_backward.1 = (bf16[32,3072]{1,0:T(8,128)(2,1)S(1)}, bf16[32,3072]{1,0:T(8,128)(2,1)S(1)}, bf16[32,3072]{1,0:T(8,128)(2,1)S(1)}, bf16[256,768]{1,0:T(8,128)(2,1)S(1)}, bf16[256,768]{1,0:T(8,128)(2,1)}) custom-call(s32[1]{0:T(128)S(6)} %copy.17.hist_len, bf16[32,3072]{1,0:T(8,128)(2,1)S(1)} %copy-done, bf16[32,3072]{1,0:T(8,128)(2,1)S(1)} %copy-done.1, ...), custom_call_target="tpu_custom_call" | custom-call | tf_op jit(solution)/shard_map/attention_backward/pallas_call | solution.py:435
  116.3 0.7 copy.18
  117.0 0.7 copy.19
  117.7 0.7 copy.20
  118.4 0.0 copy-start.4
  118.4 0.7 copy.21
  119.1 0.4 copy-done.4
  119.5 0.7 copy.22
Async XLA Ops:
  1.3 0.9 copy-start
  2.2 0.9 copy-start.1
  3.1 0.9 copy-start.2
  4.1 0.9 copy-start.3
  118.4 1.1 copy-start.4

commit v4 on v3

--- a/solution.py
+++ b/solution.py
@@ -115,7 +115,7 @@
         return zz, dist, up, (zz >= 0) & (zz < NZ)
 
     def z_copy(c, zz, way, hop):
-        to = jnp.clip(z + (1 if way == 0 else -1), 0, NZ - 1)
+        to = jnp.clip(z + 1 - 2 * way, 0, NZ - 1)
         b = zz * ny + y
         return copy(qd.at[c, b], qd.at[c, b], s_z.at[c, way, hop], r_z.at[c, way, hop], to * ny + y, h)
 
@@ -165,46 +165,78 @@
         for k in range(1, ny):
             y_copy(c, z, 0, k).start()
 
-    def gather_step(n, c):
-        zz, dist, up, ok = at_slot(n)
-
-        @pl.when((n < n_slot) & ok)
-        def _():
-            for way in range(2):
-                @pl.when((n > 0) & (up == 1 - way))
+    def event(step, e):
+        c, hop = step // 2 - e, step % 2 + 2 * e
+        return c, hop, (c >= 0) & (c < nc)
+
+    def block_at(hop, way):
+        zz = jnp.where(way == 0, z - hop, z + hop)
+        return zz, jnp.maximum(2 * hop - 1 + way, 0), (zz >= 0) & (zz < NZ) & ((hop > 0) | (way == 0))
+
+    def forward(step, e):
+        c, hop, ok = event(step, e)
+
+        @pl.when(ok & (hop == 0))
+        def _():
+            own_sends(c)
+
+        def one(way, cc):
+            zz, slot, there = block_at(hop, way)
+
+            @pl.when(ok & there & (hop > 0))
+            def _():
+                z_copy(c, zz, way, hop - 1).wait_recv()
+                to = z + 1 - 2 * way
+
+                @pl.when((to >= 0) & (to < NZ))
                 def _():
-                    z_copy(c, zz, way, dist - 1).wait_recv()
-
-                    @pl.when((z + 1 < NZ) if way == 0 else (z > 0))
-                    def _():
-                        z_copy(c, zz, way, dist).start()
-
-            @pl.when(n > 0)
-            def _():
+                    z_copy(c, zz, way, hop).start()
+
                 for k in range(1, ny):
-                    y_copy(c, zz, n, k).start()
-
-            @pl.when(n == 0)
-            def _():
-                for k in range(1, nh):
-                    for i in range(2):
-                        kv_copy(c, k, i).wait_recv()
-
-            pass1(c, zz * ny + y)
-
-        m = n - 2
-        zm, _, _, okm = at_slot(jnp.maximum(m, 0))
-
-        @pl.when((m >= 0) & okm)
-        def _():
-            def from_peer(k, cc):
-                y_copy(c, zm, m, k).wait_recv()
-                pass1(c, zm * ny + (y + ny - k) % ny)
-                return cc
-
-            lax.fori_loop(1, ny, from_peer, 0)
-
-        return c
+                    y_copy(c, zz, slot, k).start()
+
+            return cc
+
+        lax.fori_loop(0, 2, one, 0)
+
+    def own_pass(step, e):
+        c, hop, ok = event(step, e)
+
+        @pl.when(ok & (hop == 0))
+        def _():
+            for k in range(1, nh):
+                for i in range(2):
+                    kv_copy(c, k, i).wait_recv()
+
+        def one(way, cc):
+            zz, _, there = block_at(hop, way)
+
+            @pl.when(ok & there)
+            def _():
+                pass1(c, zz * ny + y)
+
+            return cc
+
+        lax.fori_loop(0, 2, one, 0)
+
+    def peer_pass(step, e):
+        c, hop, ok = event(step, e)
+
+        def one(way, cc):
+            zz, slot, there = block_at(hop, way)
+
+            @pl.when(ok & there)
+            def _():
+                def from_peer(k, ccc):
+                    y_copy(c, zz, slot, k).wait_recv()
+                    pass1(c, zz * ny + (y + ny - k) % ny)
+                    return ccc
+
+                lax.fori_loop(1, ny, from_peer, 0)
+
+            return cc
+
+        lax.fori_loop(0, 2, one, 0)
 
     def f_copy(c, k):
         return copy(fin.at[c, t], fin.at[c, t], s_f.at[c, k - 1], r_f.at[c, k - 1], (t + k) % nt, h)
@@ -315,58 +347,69 @@
         p = (h + k) % nh
         return copy(fq.at[c, band(p), :], out_q.at[:, cols(h, c)], s_c.at[c, k - 1], r_c.at[c, k - 1], t, p)
 
-    def reduce_query(c):
-        def chain(n, cc):
-            d = order(n)
-
-            @pl.when(d != z)
-            def _():
-                own_sum(c, d)
-                sz[c, d] = acc[...].astype(jnp.bfloat16)
-
-                @pl.when(z < d)
-                def _():
-                    rz_copy(c, d, 0).start()
-
-                @pl.when(z > d)
-                def _():
-                    rz_copy(c, d, 1).start()
-
-            return cc
-
-        lax.fori_loop(0, NZ, chain, 0)
+    def chain(c, n):
+        d = order(n)
+
+        @pl.when(d != z)
+        def _():
+            own_sum(c, d)
+            sz[c, d] = acc[...].astype(jnp.bfloat16)
+
+            @pl.when(z < d)
+            def _():
+                rz_copy(c, d, 0).start()
+
+            @pl.when(z > d)
+            def _():
+                rz_copy(c, d, 1).start()
+
+    def query_back(c):
         own_sum(c, z)
         fq[c] = acc[...].astype(jnp.bfloat16)
         for k in range(1, nh):
             c_copy(c, k).start()
         out_q[:, cols(h, c)] = fq[c, band(h), :]
 
-    own_sends(0)
-
-    def stage(c, cc):
-        @pl.when(c < nc)
-        def _():
-            lax.fori_loop(0, n_slot + 2, gather_step, c)
-
-        @pl.when(c + 1 < nc)
-        def _():
-            own_sends(c + 1)
-
-        @pl.when((c >= 1) & (c <= nc))
-        def _():
-            pass2(c - 1)
-
-        @pl.when(c < nc)
-        def _():
-            join(c)
-
-        @pl.when(c >= 2)
-        def _():
-            reduce_query(c - 2)
+    def stage(step, cc):
+        def each(f, at):
+            def run(i, ccc):
+                f(at, 1 - i)
+                return ccc
+
+            lax.fori_loop(0, 2, run, 0)
+
+        each(forward, step)
+        each(own_pass, step)
+
+        @pl.when(step > 0)
+        def _():
+            each(peer_pass, step - 1)
+
+        half, odd = step // 2, step % 2
+
+        @pl.when((odd == 1) & (half >= 2) & (half - 2 < nc))
+        def _():
+            pass2(half - 2)
+
+        @pl.when((odd == 0) & (half >= 2) & (half - 2 < nc))
+        def _():
+            join(half - 2)
+
+        @pl.when((half >= 3) & (half - 3 < nc))
+        def _():
+            def link(n, ccc):
+                chain(half - 3, 2 * odd + n)
+                return ccc
+
+            lax.fori_loop(0, 2, link, 0)
+
+            @pl.when(odd == 1)
+            def _():
+                query_back(half - 3)
 
         return cc
 
-    lax.fori_loop(0, nc + 2, stage, 0)
+    lax.fori_loop(0, 2 * nc + 6, stage, 0)
 
     def finish(c, cc):
         for k in range(1, nh):
@@ -463,7 +506,7 @@
             sems(nc, 2), sems(2), sems(2),
         ],
         compiler_params=pltpu.CompilerParams(
-            collective_id=0, has_side_effects=True, vmem_limit_bytes=52 * 1024 * 1024
+            collective_id=0, has_side_effects=True, vmem_limit_bytes=63 * 1024 * 1024
         ),
         name="attention_backward",
     )(hist_len, query, d_out, key_cur, value_cur, key_hist, value_hist)

time: 121 us -> 102 us (0.84)
  Pallas kernels: 111 us -> 96 us
  local copies, waits for them, and re-layouts: 7.61 us -> 4.91 us
    pallas_call x1, Pallas kernels: 111 us -> 96 us  [shards(): pl.pallas_call(functools.partial(kernel, nt, nh, nc), out_shape=(out((row...]
    unnamed x15 -> x13, local copies, waits for them, and re-layouts: 7.61 us -> 4.91 us
where the time goes in v4:
time: 102 us
  Pallas kernels  96 us (94%)
  local copies, waits for them, and re-layouts  4.91 us (5%)
  between operations  1.31 us (1%)
    pallas_call x1, Pallas kernels, shards(): pl.pallas_call(functools.partial(kernel, nt, nh, nc), out_shape=(out((row...  96 us
    unnamed x13, local copies, waits for them, and re-layouts  4.91 us

profile of v4, /device:TPU:0, one launch (start us, length us, event | category | flops | bytes accessed | tf_op | source)
XLA Modules:
  0.0 102.2 jit_solution(7458390432345172230)
XLA Ops:
  1.3 96.0 %attention_backward.1 = (bf16[32,3072]{1,0:T(8,128)(2,1)}, bf16[32,3072]{1,0:T(8,128)(2,1)}, bf16[32,3072]{1,0:T(8,128)(2,1)}, bf16[256,768]{1,0:T(8,128)(2,1)}, bf16[256,768]{1,0:T(8,128)(2,1)}) custom-call(s32[1]{0:T(128)S(6)} %copy.17.hist_len, bf16[32,3072]{1,0:T(8,128)(2,1)} %query.1, bf16[32,3072]{1,0:T(8,128)(2,1)} %d_out.1, ...), custom_call_target="tpu_custom_call" | custom-call | tf_op jit(solution)/shard_map/attention_backward/pallas_call | solution.py:478
  97.3 0.0 copy-start.3
  97.3 0.0 copy-start.2
  97.3 1.7 %copy.18 = bf16[32,3072]{1,0:T(8,128)(2,1)} copy(bf16[32,3072]{1,0:T(8,128)(2,1)} %get-tuple-element.10) | data formatting | bytes 393216
  99.0 0.0 copy-done.3
  99.0 0.0 copy-start.1
  99.0 0.7 copy.19
  99.7 0.0 copy-done.2
  99.7 0.7 copy.20
  100.4 0.0 copy-done.1
  100.4 0.0 copy-start
  100.4 0.7 copy.21
  101.1 0.4 copy-done
  101.5 0.7 copy.22
Async XLA Ops:
  97.3 1.7 %copy-start.3 = (bf16[32,3072]{1,0:T(8,128)(2,1)S(1)}, bf16[32,3072]{1,0:T(8,128)(2,1)}, u32[]{:S(2)}) copy-start(bf16[32,3072]{1,0:T(8,128)(2,1)} %get-tuple-element.11) | copy-start | bytes 589828
  97.3 2.4 %copy-start.2 = (bf16[32,3072]{1,0:T(8,128)(2,1)S(1)}, bf16[32,3072]{1,0:T(8,128)(2,1)}, u32[]{:S(2)}) copy-start(bf16[32,3072]{1,0:T(8,128)(2,1)} %get-tuple-element.12) | copy-start | bytes 589828
  99.0 1.4 %copy-start.1 = (bf16[256,768]{1,0:T(8,128)(2,1)S(1)}, bf16[256,768]{1,0:T(8,128)(2,1)}, u32[]{:S(2)}) copy-start(bf16[256,768]{1,0:T(8,128)(2,1)} %get-tuple-element.13) | copy-start | bytes 1179652
  100.4 1.1 %copy-start = (bf16[256,768]{1,0:T(8,128)(2,1)S(1)}, bf16[256,768]{1,0:T(8,128)(2,1)}, u32[]{:S(2)}) copy-start(bf16[256,768]{1,0:T(8,128)(2,1)} %get-tuple-element.14) | copy-start | bytes 1179652

commit v5 on v4

--- a/solution.py
+++ b/solution.py
@@ -15,10 +15,10 @@
 
 
 def kernel(
-    nt, nh, nc,
+    nt, nh, nc, keep,
     hist_len, query, d_out, key_cur, value_cur, key_hist, value_hist,
     out_q, out_k, out_v, out_kh, out_vh,
-    qd, kv, dkv, dq, ry, rz, sz, st, st_in, fin, acc, fq, fkv, bias,
+    qd, kv, dkv, dq, ry, rz, sz, st, st_in, fin, acc, fq, fkv, bias, kt, kept,
     s_a, r_a, s_kv, r_kv, s_z, r_z, s_y, r_y, s_st, r_st, s_f, r_f,
     s_ry, r_ry, s_rz, r_rz, s_b, r_b, s_c, r_c, s_own, s_hist, s_oc,
 ):
@@ -140,6 +140,9 @@
             g = nt_dot(kv[1, :, hc], qd[c, b, 1, :, lc])
             m = jnp.max(s, axis=0, keepdims=True)
             w = jnp.exp2(s - m)
+            if keep:
+                kept[c, b, 0, i] = w
+                kept[c, b, 1, i] = g
             st[c, b, i : i + 1, :] = m
             st[c, b, hpc + i : hpc + i + 1, :] = jnp.sum(w, axis=0, keepdims=True)
             st[c, b, 2 * hpc + i : 2 * hpc + i + 1, :] = jnp.sum(w * g, axis=0, keepdims=True)
@@ -207,6 +210,7 @@
             for k in range(1, nh):
                 for i in range(2):
                     kv_copy(c, k, i).wait_recv()
+            kt[part(c), :] = kv[0, :, part(c)].T
 
         def one(way, cc):
             zz, _, there = block_at(hop, way)
@@ -289,23 +293,24 @@
                     q = jnp.concatenate([qd[c, b, 0, :, lc], qd[c, b + 1, 0, :, lc]], axis=0)
                     do = jnp.concatenate([qd[c, b, 1, :, lc], qd[c, b + 1, 1, :, lc]], axis=0)
 
-                    def stat(r):
-                        row = r * hpc + i
-                        return jnp.concatenate(
-                            [fin[c, b, row : row + 1, :], fin[c, b + 1, row : row + 1, :]], axis=1
-                        )
-
-                    s = nt_dot(key, q) * scale2 + bias[...]
-                    g = nt_dot(val, do)
-                    p = jnp.exp2(s - stat(0)) * stat(1)
-                    sg = (p * scale * (g - stat(2))).astype(jnp.bfloat16)
+                    def row(ref, r):
+                        at = slice(r * hpc + i, r * hpc + i + 1)
+                        return jnp.concatenate([ref[c, b, at, :], ref[c, b + 1, at, :]], axis=1)
+
+                    if keep:
+                        share = jnp.exp2(row(st, 0) - row(fin, 0)) * row(fin, 1)
+                        p = jnp.concatenate([kept[c, b, 0, i], kept[c, b + 1, 0, i]], axis=1) * share
+                        g = jnp.concatenate([kept[c, b, 1, i], kept[c, b + 1, 1, i]], axis=1)
+                    else:
+                        s = nt_dot(key, q) * scale2 + bias[...]
+                        g = nt_dot(val, do)
+                        p = jnp.exp2(s - row(fin, 0)) * row(fin, 1)
+                    sg = (p * scale * (g - row(fin, 2))).astype(jnp.bfloat16)
                     dkv[0, :, hc] += jnp.dot(sg, q, preferred_element_type=jnp.float32)
                     dkv[1, :, hc] += jnp.dot(p.astype(jnp.bfloat16), do, preferred_element_type=jnp.float32)
-                    term = lax.dot_general(
-                        sg, key, (((0,), (0,)), ((), ())), preferred_element_type=jnp.float32
-                    ).astype(jnp.bfloat16)
-                    dq[c, b, :, lc] = term[:cur]
-                    dq[c, b + 1, :, lc] = term[cur:]
+                    term = jnp.dot(kt[hc, :], sg, preferred_element_type=jnp.float32).astype(jnp.bfloat16)
+                    dq[c, b, lc, :] = term[:, :cur]
+                    dq[c, b + 1, lc, :] = term[:, cur:]
                 return ccc
 
             lax.fori_loop(0, ny // 2, pair, 0)
@@ -365,7 +370,7 @@
 
     def query_back(c):
         own_sum(c, z)
-        fq[c] = acc[...].astype(jnp.bfloat16)
+        fq[c] = acc[...].T.astype(jnp.bfloat16)
         for k in range(1, nh):
             c_copy(c, k).start()
         out_q[:, cols(h, c)] = fq[c, band(h), :]
@@ -467,6 +472,10 @@
     n_k = cur + key_hist.shape[0]
     nc = 3 if feat % (3 * HS) == 0 else 1
     wide = feat // nc
+    store = (nc, nt, 2, wide // HS, n_k, cur)
+    keep = math.prod(store) * 4 <= 24 * 1024 * 1024
+    if not keep:
+        store = (SLOTS, HS)
     hbm = pl.BlockSpec(memory_space=pl.ANY)
     bf, f32 = jnp.bfloat16, jnp.float32
     vmem = pl.BlockSpec(memory_space=pltpu.VMEM)
@@ -476,7 +485,7 @@
 
     out = jax.ShapeDtypeStruct
     return pl.pallas_call(
-        functools.partial(kernel, nt, nh, nc),
+        functools.partial(kernel, nt, nh, nc, keep),
         out_shape=(
             out((rows, width), bf), out((rows, width), bf), out((rows, width), bf),
             out(key_hist.shape, bf), out(value_hist.shape, bf),
@@ -487,17 +496,19 @@
             pltpu.VMEM((nc, nt, 2, cur, wide), bf),
             pltpu.VMEM((2, n_k, feat), bf),
             pltpu.VMEM((2, n_k, feat), f32),
-            pltpu.VMEM((nc, nt, cur, wide), bf),
-            pltpu.VMEM((nc, NZ, ny - 1, cur, wide), bf),
-            pltpu.VMEM((nc, 2, NZ, cur, wide), bf),
-            pltpu.VMEM((nc, NZ, cur, wide), bf),
+            pltpu.VMEM((nc, nt, wide, cur), bf),
+            pltpu.VMEM((nc, NZ, ny - 1, wide, cur), bf),
+            pltpu.VMEM((nc, 2, NZ, wide, cur), bf),
+            pltpu.VMEM((nc, NZ, wide, cur), bf),
             pltpu.VMEM((nc, nt, SLOTS, cur), f32),
             pltpu.VMEM((nc, nt, SLOTS, cur), f32),
             pltpu.VMEM((nc, nt, SLOTS, cur), f32),
-            pltpu.VMEM((cur, wide), f32),
+            pltpu.VMEM((wide, cur), f32),
             pltpu.VMEM((nc, cur, wide), bf),
             pltpu.VMEM((2, cur, feat), bf),
             pltpu.VMEM((n_k, 2 * cur), f32),
+            pltpu.VMEM((feat, n_k), bf),
+            pltpu.VMEM(store, f32),
             sems(nc, nh - 1, 2), sems(nc, nh - 1, 2), sems(nc, nh - 1, 2), sems(nc, nh - 1, 2),
             sems(nc, 2, NZ), sems(nc, 2, NZ), sems(nc, 2 * NZ - 1, ny - 1), sems(nc, 2 * NZ - 1, ny - 1),
             sems(nc, nt), sems(nc, nt), sems(nc, nt - 1), sems(nc, nt - 1),

time: 102 us -> 99.8 us (0.978)
  Pallas kernels: 96 us -> 93.3 us
    pallas_call x1, Pallas kernels: 96 us -> 93.3 us  [shards(): pl.pallas_call(functools.partial(kernel, nt, nh, nc, keep), out_shape=(ou...]
where the time goes in v5:
time: 99.8 us; the launch traced here: 99.6 us
  Pallas kernels  93.3 us (93%)
  local copies, waits for them, and re-layouts  4.91 us (5%)
  between operations  1.31 us (1%)
    pallas_call x1, Pallas kernels, shards(): pl.pallas_call(functools.partial(kernel, nt, nh, nc, keep), out_shape=(ou...  93.3 us
    unnamed x13, local copies, waits for them, and re-layouts  4.91 us

profile of v5, /device:TPU:0, one launch (start us, length us, event | category | flops | bytes accessed | tf_op | source)
XLA Modules:
  0.0 99.6 jit_solution(14239358680166605365)
XLA Ops:
  1.3 93.3 %attention_backward.1 = (bf16[32,3072]{1,0:T(8,128)(2,1)}, bf16[32,3072]{1,0:T(8,128)(2,1)}, bf16[32,3072]{1,0:T(8,128)(2,1)}, bf16[256,768]{1,0:T(8,128)(2,1)}, bf16[256,768]{1,0:T(8,128)(2,1)}) custom-call(s32[1]{0:T(128)S(6)} %copy.17.hist_len, bf16[32,3072]{1,0:T(8,128)(2,1)} %query.1, bf16[32,3072]{1,0:T(8,128)(2,1)} %d_out.1, ...), custom_call_target="tpu_custom_call" | custom-call | tf_op jit(solution)/shard_map/attention_backward/pallas_call | solution.py:487
  94.6 0.0 copy-start.3
  94.6 0.0 copy-start.2
  94.7 1.7 %copy.18 = bf16[32,3072]{1,0:T(8,128)(2,1)} copy(bf16[32,3072]{1,0:T(8,128)(2,1)} %get-tuple-element.10) | data formatting | bytes 393216
  96.3 0.0 copy-done.3
  96.3 0.0 copy-start.1
  96.3 0.7 copy.19
  97.0 0.0 copy-done.2
  97.0 0.7 copy.20
  97.7 0.0 copy-done.1
  97.7 0.0 copy-start
  97.7 0.7 copy.21
  98.4 0.4 copy-done
  98.8 0.7 copy.22
Async XLA Ops:
  94.6 1.7 %copy-start.3 = (bf16[32,3072]{1,0:T(8,128)(2,1)S(1)}, bf16[32,3072]{1,0:T(8,128)(2,1)}, u32[]{:S(2)}) copy-start(bf16[32,3072]{1,0:T(8,128)(2,1)} %get-tuple-element.11) | copy-start | bytes 589828
  94.6 2.4 %copy-start.2 = (bf16[32,3072]{1,0:T(8,128)(2,1)S(1)}, bf16[32,3072]{1,0:T(8,128)(2,1)}, u32[]{:S(2)}) copy-start(bf16[32,3072]{1,0:T(8,128)(2,1)} %get-tuple-element.12) | copy-start | bytes 589828
  96.3 1.4 %copy-start.1 = (bf16[256,768]{1,0:T(8,128)(2,1)S(1)}, bf16[256,768]{1,0:T(8,128)(2,1)}, u32[]{:S(2)}) copy-start(bf16[256,768]{1,0:T(8,128)(2,1)} %get-tuple-element.13) | copy-start | bytes 1179652
  97.7 1.1 %copy-start = (bf16[256,768]{1,0:T(8,128)(2,1)S(1)}, bf16[256,768]{1,0:T(8,128)(2,1)}, u32[]{:S(2)}) copy-start(bf16[256,768]{1,0:T(8,128)(2,1)} %get-tuple-element.14) | copy-start | bytes 1179652

commit v6 on v5

--- a/solution.py
+++ b/solution.py
@@ -463,6 +463,450 @@
     lax.fori_loop(0, nc, finish, 0)
 
 
+def kernel_split(
+    nt, nh, nc,
+    hist_len, query, d_out, key_cur, value_cur, key_hist, value_hist,
+    out_q, out_k, out_v, out_kh, out_vh,
+    qd, kv, dkv, dq, rz, sz, st, st_in, fin, acc, fq, fkv, bias, kt, kept, lens,
+    s_a, r_a, s_kv, r_kv, s_z, r_z, s_st, r_st, s_f, r_f,
+    s_rz, r_rz, s_b, r_b, s_c, r_c, s_own, s_hist, s_oc, s_h, r_h, s_hb, r_hb, s_l, r_l,
+):
+    ny = nt // NZ
+    rows = query.shape[0]
+    feat = query.shape[1] // nh
+    part_w = feat // ny
+    heads = part_w // HS
+    hpc = heads // nc
+    width = hpc * HS
+    ng = nh * ny
+    cur = rows * ng
+    hist = key_hist.shape[0]
+    n_k = kv.shape[1]
+    scale = 1.0 / math.sqrt(HS)
+    scale2 = scale * math.log2(math.e)
+    t, h = lax.axis_index("tm"), lax.axis_index("head")
+    z, y = t // ny, t % ny
+    g = y * nh + h
+
+    def copy(src, dst, ss, rs, tm, hd):
+        return pltpu.make_async_remote_copy(
+            src_ref=src, dst_ref=dst, send_sem=ss, recv_sem=rs,
+            device_id=(tm, hd), device_id_type=MESH,
+        )
+
+    def peer(k):
+        p = (g + k) % ng
+        return p, p // nh, p % nh
+
+    def cols(py, ph, c):
+        return pl.ds(pl.multiple_of(ph * feat + py * part_w + c * width, HS), width)
+
+    def hist_cols(py, c):
+        return pl.ds(pl.multiple_of(py * part_w + c * width, HS), width)
+
+    def hist_rows(py):
+        return pl.ds(pl.multiple_of(cur + py * hist, HS), hist)
+
+    def part(c):
+        return pl.ds(pl.multiple_of(c * width, HS), width)
+
+    def band(i):
+        return pl.ds(pl.multiple_of(i * rows, rows), rows)
+
+    def own_copy(c, i):
+        src = (query, d_out)[i]
+        return pltpu.make_async_copy(src.at[:, cols(y, h, c)], qd.at[c, z, i, band(g), :], s_own.at[c, i])
+
+    def own_kv(i):
+        src = (key_cur, value_cur)[i]
+        return pltpu.make_async_copy(
+            src.at[:, pl.ds(pl.multiple_of(h * feat + y * part_w, HS), part_w)], kv.at[i, band(g), :], s_oc.at[i]
+        )
+
+    def hist_copy(i):
+        src = (key_hist, value_hist)[i]
+        return pltpu.make_async_copy(
+            src.at[:, pl.ds(pl.multiple_of(y * part_w, HS), part_w)], kv.at[i, hist_rows(y), :], s_hist.at[i]
+        )
+
+    def a_copy(c, k, i):
+        src = (query, d_out)[i]
+        p, py, ph = peer(k)
+        return copy(
+            src.at[:, cols(py, ph, c)], qd.at[c, z, i, band(g), :],
+            s_a.at[c, k - 1, i], r_a.at[c, k - 1, i], z * ny + py, ph,
+        )
+
+    def kv_copy(c, k, i):
+        src = (key_cur, value_cur)[i]
+        p, py, ph = peer(k)
+        return copy(
+            src.at[:, cols(py, ph, c)], kv.at[i, band(g), part(c)],
+            s_kv.at[c, k - 1, i], r_kv.at[c, k - 1, i], z * ny + py, ph,
+        )
+
+    def h_copy(c, k, i):
+        src = (key_hist, value_hist)[i]
+        py = (y + k) % ny
+        return copy(
+            src.at[:, hist_cols(py, c)], kv.at[i, hist_rows(y), part(c)],
+            s_h.at[c, k - 1, i], r_h.at[c, k - 1, i], z * ny + py, h,
+        )
+
+    def l_copy(k):
+        py = (y + k) % ny
+        return copy(lens.at[y], lens.at[y], s_l.at[k - 1], r_l.at[k - 1], z * ny + py, h)
+
+    for i in range(2):
+        for c in range(nc):
+            own_copy(c, i).start()
+        own_kv(i).start()
+        hist_copy(i).start()
+
+    barrier = pltpu.get_barrier_semaphore()
+    lens[y] = jnp.full(lens.shape[1:], hist_len[0], jnp.int32)
+    for k in range(1, NZ):
+        to = (z + k) % NZ
+        pl.semaphore_signal(barrier, inc=1, device_id=(to * ny + y, h), device_id_type=MESH)
+    for k in range(1, ng):
+        _, py, ph = peer(k)
+        pl.semaphore_signal(barrier, inc=1, device_id=(z * ny + py, ph), device_id_type=MESH)
+    pl.semaphore_wait(barrier, NZ + ng - 2)
+
+    for k in range(1, ny):
+        l_copy(k).start()
+
+    def exchange(c, cc):
+        for i in range(2):
+            for k in range(1, ng):
+                a_copy(c, k, i).start()
+        for i in range(2):
+            for k in range(1, ng):
+                kv_copy(c, k, i).start()
+            for k in range(1, ny):
+                h_copy(c, k, i).start()
+        return cc
+
+    lax.fori_loop(0, nc, exchange, 0)
+    st[...] = jnp.zeros_like(st)
+    dkv[...] = jnp.zeros_like(dkv)
+    for k in range(1, ny):
+        l_copy(k).wait_recv()
+    bias[:cur, :] = jnp.zeros((cur, cur), jnp.float32)
+    slot_row = lax.broadcasted_iota(jnp.int32, (hist, cur), 0)
+    for j in range(ny):
+        bias[cur + j * hist : cur + (j + 1) * hist, :] = jnp.where(slot_row < lens[j, :1, :], 0.0, -1e30)
+    for i in range(2):
+        own_kv(i).wait()
+        hist_copy(i).wait()
+
+    def z_copy(c, zz, way, hop):
+        to = jnp.clip(z + 1 - 2 * way, 0, NZ - 1)
+        return copy(qd.at[c, zz], qd.at[c, zz], s_z.at[c, way, hop], r_z.at[c, way, hop], to * ny + y, h)
+
+    def st_copy(c, b):
+        return copy(st.at[c, b], st_in.at[c, z], s_st.at[c, b], r_st.at[c, z], b * ny + y, h)
+
+    def head_cols(i):
+        return pl.ds(pl.multiple_of(i * HS, HS), HS)
+
+    def nt_dot(a, b):
+        return lax.dot_general(a, b, (((1,), (1,)), ((), ())), preferred_element_type=jnp.float32)
+
+    def pass1(c, b):
+        for i in range(hpc):
+            hc, lc = head_cols(c * hpc + i), slice(i * HS, (i + 1) * HS)
+            s = nt_dot(kv[0, :, hc], qd[c, b, 0, :, lc]) * scale2 + bias[...]
+            gs = nt_dot(kv[1, :, hc], qd[c, b, 1, :, lc])
+            m = jnp.max(s, axis=0, keepdims=True)
+            w = jnp.exp2(s - m)
+            kept[c, b, 0, i] = w
+            kept[c, b, 1, i] = gs
+            st[c, b, i : i + 1, :] = m
+            st[c, b, hpc + i : hpc + i + 1, :] = jnp.sum(w, axis=0, keepdims=True)
+            st[c, b, 2 * hpc + i : 2 * hpc + i + 1, :] = jnp.sum(w * gs, axis=0, keepdims=True)
+
+        @pl.when(b != z)
+        def _():
+            st_copy(c, b).start()
+
+    def own_sends(c):
+        for i in range(2):
+            own_copy(c, i).wait()
+            for k in range(1, ng):
+                a_copy(c, k, i).wait_recv()
+
+        @pl.when(z + 1 < NZ)
+        def _():
+            z_copy(c, z, 0, 0).start()
+
+        @pl.when(z > 0)
+        def _():
+            z_copy(c, z, 1, 0).start()
+
+    def event(step, e):
+        c, hop = step // 2 - e, step % 2 + 2 * e
+        return c, hop, (c >= 0) & (c < nc)
+
+    def block_at(hop, way):
+        zz = jnp.where(way == 0, z - hop, z + hop)
+        return zz, (zz >= 0) & (zz < NZ) & ((hop > 0) | (way == 0))
+
+    def forward(step, e):
+        c, hop, ok = event(step, e)
+
+        @pl.when(ok & (hop == 0))
+        def _():
+            own_sends(c)
+
+        def one(way, cc):
+            zz, there = block_at(hop, way)
+
+            @pl.when(ok & there & (hop > 0))
+            def _():
+                z_copy(c, zz, way, hop - 1).wait_recv()
+                to = z + 1 - 2 * way
+
+                @pl.when((to >= 0) & (to < NZ))
+                def _():
+                    z_copy(c, zz, way, hop).start()
+
+            return cc
+
+        lax.fori_loop(0, 2, one, 0)
+
+    def own_pass(step, e):
+        c, hop, ok = event(step, e)
+
+        @pl.when(ok & (hop == 0))
+        def _():
+            for i in range(2):
+                for k in range(1, ng):
+                    kv_copy(c, k, i).wait_recv()
+                for k in range(1, ny):
+                    h_copy(c, k, i).wait_recv()
+            kt[part(c), :] = kv[0, :, part(c)].T
+
+        def one(way, cc):
+            zz, there = block_at(hop, way)
+
+            @pl.when(ok & there)
+            def _():
+                pass1(c, zz)
+
+            return cc
+
+        lax.fori_loop(0, 2, one, 0)
+
+    def f_copy(c, k):
+        to = (z + k) % NZ
+        return copy(fin.at[c, z], fin.at[c, z], s_f.at[c, k - 1], r_f.at[c, k - 1], to * ny + y, h)
+
+    def join(c):
+        st_in[c, z] = st[c, z]
+        for k in range(1, NZ):
+            src = (z + NZ - k) % NZ
+            copy(st.at[c, z], st_in.at[c, src], s_st.at[c, src], r_st.at[c, src], src * ny + y, h).wait_recv()
+        local = st_in[c]
+        top = jnp.max(local[:, :hpc], axis=0)
+        back = jnp.exp2(local[:, :hpc] - top[None])
+        total = jnp.sum(local[:, hpc : 2 * hpc] * back, axis=0)
+        dots = jnp.sum(local[:, 2 * hpc : 3 * hpc] * back, axis=0)
+        fin[c, z] = jnp.zeros_like(fin[c, z])
+        fin[c, z, :hpc, :] = top
+        fin[c, z, hpc : 2 * hpc, :] = 1.0 / total
+        fin[c, z, 2 * hpc : 3 * hpc, :] = dots / total
+        for k in range(1, NZ):
+            f_copy(c, k).start()
+
+    def order(i):
+        return jnp.where(z < NZ // 2, NZ - 1 - i, i)
+
+    def b_copy(c, k, i):
+        p, py, ph = peer(k)
+        dst = (out_k, out_v)[i]
+        return copy(
+            fkv.at[i, band(p), part(c)], dst.at[:, cols(y, h, c)],
+            s_b.at[c, k - 1, i], r_b.at[c, k - 1, i], z * ny + py, ph,
+        )
+
+    def hb_copy(c, k, i):
+        py = (y + k) % ny
+        dst = (out_kh, out_vh)[i]
+        return copy(
+            fkv.at[i, hist_rows(py), part(c)], dst.at[:, hist_cols(y, c)],
+            s_hb.at[c, k - 1, i], r_hb.at[c, k - 1, i], z * ny + py, h,
+        )
+
+    def pass2(c):
+        for k in range(1, NZ):
+            f_copy(c, k).wait_recv()
+
+        def group(n, cc):
+            d = order(n)
+            for i in range(hpc):
+                hc, lc = head_cols(c * hpc + i), slice(i * HS, (i + 1) * HS)
+                q, do = qd[c, d, 0, :, lc], qd[c, d, 1, :, lc]
+
+                def row(ref, r):
+                    return ref[c, d, r * hpc + i : r * hpc + i + 1, :]
+
+                share = jnp.exp2(row(st, 0) - row(fin, 0)) * row(fin, 1)
+                p = kept[c, d, 0, i] * share
+                sg = (p * scale * (kept[c, d, 1, i] - row(fin, 2))).astype(jnp.bfloat16)
+                dkv[0, :, hc] += jnp.dot(sg, q, preferred_element_type=jnp.float32)
+                dkv[1, :, hc] += jnp.dot(p.astype(jnp.bfloat16), do, preferred_element_type=jnp.float32)
+                dq[c, d, lc, :] = jnp.dot(kt[hc, :], sg, preferred_element_type=jnp.float32).astype(jnp.bfloat16)
+            return cc
+
+        lax.fori_loop(0, NZ, group, 0)
+        for i in range(2):
+            fkv[i, :, part(c)] = dkv[i, :, part(c)].astype(jnp.bfloat16)
+            for k in range(1, ny):
+                hb_copy(c, k, i).start()
+            for k in range(1, ng):
+                b_copy(c, k, i).start()
+            out = (out_k, out_v)[i]
+            out[:, cols(y, h, c)] = fkv[i, band(g), part(c)]
+            out = (out_kh, out_vh)[i]
+            out[:, hist_cols(y, c)] = fkv[i, hist_rows(y), part(c)]
+
+    def rz_copy(c, d, way):
+        to = jnp.clip(z + (1 if way == 0 else -1), 0, NZ - 1)
+        return copy(sz.at[c, d], rz.at[c, way, d], s_rz.at[c, way, d], r_rz.at[c, way, d], to * ny + y, h)
+
+    def own_sum(c, d):
+        acc[...] = dq[c, d].astype(jnp.float32)
+
+        @pl.when((z <= d) & (z > 0))
+        def _():
+            rz_copy(c, d, 0).wait_recv()
+            acc[...] += rz[c, 0, d].astype(jnp.float32)
+
+        @pl.when((z >= d) & (z < NZ - 1))
+        def _():
+            rz_copy(c, d, 1).wait_recv()
+            acc[...] += rz[c, 1, d].astype(jnp.float32)
+
+    def c_copy(c, k):
+        p, py, ph = peer(k)
+        return copy(
+            fq.at[c, band(p), :], out_q.at[:, cols(y, h, c)], s_c.at[c, k - 1], r_c.at[c, k - 1], z * ny + py, ph
+        )
+
+    def chain(c, n):
+        d = order(n)
+
+        @pl.when(d != z)
+        def _():
+            own_sum(c, d)
+            sz[c, d] = acc[...].astype(jnp.bfloat16)
+
+            @pl.when(z < d)
+            def _():
+                rz_copy(c, d, 0).start()
+
+            @pl.when(z > d)
+            def _():
+                rz_copy(c, d, 1).start()
+
+    def query_back(c):
+        own_sum(c, z)
+        fq[c] = acc[...].T.astype(jnp.bfloat16)
+        for k in range(1, ng):
+            c_copy(c, k).start()
+        out_q[:, cols(y, h, c)] = fq[c, band(g), :]
+
+    def stage(step, cc):
+        def each(f, at):
+            def run(i, ccc):
+                f(at, 1 - i)
+                return ccc
+
+            lax.fori_loop(0, 2, run, 0)
+
+        each(forward, step)
+        each(own_pass, step)
+
+        half, odd = step // 2, step % 2
+
+        @pl.when((odd == 0) & (half >= 2) & (half - 2 < nc))
+        def _():
+            pass2(half - 2)
+
+        @pl.when((odd == 1) & (half >= 1) & (half - 1 < nc))
+        def _():
+            join(half - 1)
+
+        late = (step - 5) // 2
+
+        @pl.when((step >= 5) & (late < nc))
+        def _():
+            def link(n, ccc):
+                chain(late, 2 * (1 - odd) + n)
+                return ccc
+
+            lax.fori_loop(0, 2, link, 0)
+
+            @pl.when(odd == 0)
+            def _():
+                query_back(late)
+
+        return cc
+
+    lax.fori_loop(0, 2 * nc + 5, stage, 0)
+
+    def finish(c, cc):
+        for k in range(1, ng):
+            c_copy(c, k).wait()
+            for i in range(2):
+                b_copy(c, k, i).wait()
+                a_copy(c, k, i).wait_send()
+                kv_copy(c, k, i).wait_send()
+        for k in range(1, ny):
+            for i in range(2):
+                hb_copy(c, k, i).wait()
+                h_copy(c, k, i).wait_send()
+        for k in range(1, NZ):
+            f_copy(c, k).wait_send()
+            st_copy(c, (z + k) % NZ).wait_send()
+
+        def sent(hop, ccc):
+            def one(way, cccc):
+                zz, there = block_at(hop, way)
+                to = z + 1 - 2 * way
+                there = there | ((hop == 0) & (way == 1))
+
+                @pl.when(there & (to >= 0) & (to < NZ))
+                def _():
+                    z_copy(c, zz, way, hop).wait_send()
+
+                return cccc
+
+            lax.fori_loop(0, 2, one, 0)
+            return ccc
+
+        lax.fori_loop(0, NZ, sent, 0)
+
+        def reduced(d, ccc):
+            @pl.when(z < d)
+            def _():
+                rz_copy(c, d, 0).wait_send()
+
+            @pl.when(z > d)
+            def _():
+                rz_copy(c, d, 1).wait_send()
+
+            return ccc
+
+        lax.fori_loop(0, NZ, reduced, 0)
+        return cc
+
+    for k in range(1, ny):
+        l_copy(k).wait_send()
+    lax.fori_loop(0, nc, finish, 0)
+
+
 def shards(query, key_cur, value_cur, d_out, key_hist, value_hist, hist_len):
     nt, nh = lax.axis_size("tm"), lax.axis_size("head")
     ny = nt // NZ
@@ -484,6 +928,51 @@
         return pltpu.SemaphoreType.DMA(dims)
 
     out = jax.ShapeDtypeStruct
+    out_shape = (
+        out((rows, width), bf), out((rows, width), bf), out((rows, width), bf),
+        out(key_hist.shape, bf), out(value_hist.shape, bf),
+    )
+    if feat % (ny * HS) == 0:
+        ng, part_w, hist = nh * ny, feat // ny, key_hist.shape[0]
+        cur, n_k = rows * ng, rows * ng + ny * hist
+        nc = part_w // HS
+        wide = HS
+        return pl.pallas_call(
+            functools.partial(kernel_split, nt, nh, nc),
+            out_shape=out_shape,
+            in_specs=[pl.BlockSpec(memory_space=pltpu.SMEM)] + [hbm] * 6,
+            out_specs=(vmem,) * 5,
+            scratch_shapes=[
+                pltpu.VMEM((nc, NZ, 2, cur, wide), bf),
+                pltpu.VMEM((2, n_k, part_w), bf),
+                pltpu.VMEM((2, n_k, part_w), f32),
+                pltpu.VMEM((nc, NZ, wide, cur), bf),
+                pltpu.VMEM((nc, 2, NZ, wide, cur), bf),
+                pltpu.VMEM((nc, NZ, wide, cur), bf),
+                pltpu.VMEM((nc, NZ, SLOTS, cur), f32),
+                pltpu.VMEM((nc, NZ, SLOTS, cur), f32),
+                pltpu.VMEM((nc, NZ, SLOTS, cur), f32),
+                pltpu.VMEM((wide, cur), f32),
+                pltpu.VMEM((nc, cur, wide), bf),
+                pltpu.VMEM((2, n_k, part_w), bf),
+                pltpu.VMEM((n_k, cur), f32),
+                pltpu.VMEM((part_w, n_k), bf),
+                pltpu.VMEM((nc, NZ, 2, 1, n_k, cur), f32),
+                pltpu.VMEM((ny, SLOTS, cur), jnp.int32),
+                sems(nc, ng - 1, 2), sems(nc, ng - 1, 2), sems(nc, ng - 1, 2), sems(nc, ng - 1, 2),
+                sems(nc, 2, NZ), sems(nc, 2, NZ),
+                sems(nc, NZ), sems(nc, NZ), sems(nc, NZ - 1), sems(nc, NZ - 1),
+                sems(nc, 2, NZ), sems(nc, 2, NZ),
+                sems(nc, ng - 1, 2), sems(nc, ng - 1, 2), sems(nc, ng - 1), sems(nc, ng - 1),
+                sems(nc, 2), sems(2), sems(2),
+                sems(nc, ny - 1, 2), sems(nc, ny - 1, 2), sems(nc, ny - 1, 2), sems(nc, ny - 1, 2),
+                sems(ny - 1), sems(ny - 1),
+            ],
+            compiler_params=pltpu.CompilerParams(
+                collective_id=0, has_side_effects=True, vmem_limit_bytes=63 * 1024 * 1024
+            ),
+            name="attention_backward_split",
+        )(hist_len, query, d_out, key_cur, value_cur, key_hist, value_hist)
     return pl.pallas_call(
         functools.partial(kernel, nt, nh, nc, keep),
         out_shape=(

time: 99.8 us -> 96.8 us (0.970)
  Pallas kernels: 93.3 us -> 90.3 us
    pallas_call x1, Pallas kernels: 93.3 us -> 90.3 us  [shards(): pl.pallas_call(functools.partial(kernel_split, nt, nh, nc), out_shape=out...]
where the time goes in v6:
time: 96.8 us; the launch traced here: 96.6 us
  Pallas kernels  90.3 us (93%)
  local copies, waits for them, and re-layouts  4.91 us (5%)
  between operations  1.31 us (1%)
    pallas_call x1, Pallas kernels, shards(): pl.pallas_call(functools.partial(kernel_split, nt, nh, nc), out_shape=out...  90.3 us
    unnamed x13, local copies, waits for them, and re-layouts  4.91 us

profile of v6, /device:TPU:0, one launch (start us, length us, event | category | flops | bytes accessed | tf_op | source)
XLA Modules:
  0.0 96.6 jit_solution(6681353831803760390)
XLA Ops:
  1.3 90.3 %attention_backward_split.1 = (bf16[32,3072]{1,0:T(8,128)(2,1)}, bf16[32,3072]{1,0:T(8,128)(2,1)}, bf16[32,3072]{1,0:T(8,128)(2,1)}, bf16[256,768]{1,0:T(8,128)(2,1)}, bf16[256,768]{1,0:T(8,128)(2,1)}) custom-call(s32[1]{0:T(128)S(6)} %copy.17.hist_len, bf16[32,3072]{1,0:T(8,128)(2,1)} %query.1, bf16[32,3072]{1,0:T(8,128)(2,1)} %d_out.1, ...), custom_call_target="tpu_custom_call" | custom-call | tf_op jit(solution)/shard_map/attention_backward_split/pallas_call | solution.py:940
  91.6 0.0 copy-start.3
  91.6 0.0 copy-start.2
  91.7 1.7 %copy.18 = bf16[32,3072]{1,0:T(8,128)(2,1)} copy(bf16[32,3072]{1,0:T(8,128)(2,1)} %get-tuple-element.10) | data formatting | bytes 393216
  93.3 0.0 copy-done.3
  93.3 0.0 copy-start.1
  93.3 0.7 copy.19
  94.0 0.0 copy-done.2
  94.0 0.7 copy.20
  94.7 0.0 copy-done.1
  94.7 0.0 copy-start
  94.7 0.7 copy.21
  95.4 0.4 copy-done
  95.8 0.7 copy.22
Async XLA Ops:
  91.6 1.7 %copy-start.3 = (bf16[32,3072]{1,0:T(8,128)(2,1)S(1)}, bf16[32,3072]{1,0:T(8,128)(2,1)}, u32[]{:S(2)}) copy-start(bf16[32,3072]{1,0:T(8,128)(2,1)} %get-tuple-element.11) | copy-start | bytes 589828
  91.6 2.4 %copy-start.2 = (bf16[32,3072]{1,0:T(8,128)(2,1)S(1)}, bf16[32,3072]{1,0:T(8,128)(2,1)}, u32[]{:S(2)}) copy-start(bf16[32,3072]{1,0:T(8,128)(2,1)} %get-tuple-element.12) | copy-start | bytes 589828
  93.3 1.4 %copy-start.1 = (bf16[256,768]{1,0:T(8,128)(2,1)S(1)}, bf16[256,768]{1,0:T(8,128)(2,1)}, u32[]{:S(2)}) copy-start(bf16[256,768]{1,0:T(8,128)(2,1)} %get-tuple-element.13) | copy-start | bytes 1179652
  94.7 1.1 %copy-start = (bf16[256,768]{1,0:T(8,128)(2,1)S(1)}, bf16[256,768]{1,0:T(8,128)(2,1)}, u32[]{:S(2)}) copy-start(bf16[256,768]{1,0:T(8,128)(2,1)} %get-tuple-element.14) | copy-start | bytes 1179652

commit v7 on v6

--- a/solution.py
+++ b/solution.py
@@ -501,6 +501,9 @@
     def cols(py, ph, c):
         return pl.ds(pl.multiple_of(ph * feat + py * part_w + c * width, HS), width)
 
+    def wide_cols(py, ph):
+        return pl.ds(pl.multiple_of(ph * feat + py * part_w, HS), part_w)
+
     def hist_cols(py, c):
         return pl.ds(pl.multiple_of(py * part_w + c * width, HS), width)
 
@@ -513,9 +516,9 @@
     def band(i):
         return pl.ds(pl.multiple_of(i * rows, rows), rows)
 
-    def own_copy(c, i):
+    def own_copy(i):
         src = (query, d_out)[i]
-        return pltpu.make_async_copy(src.at[:, cols(y, h, c)], qd.at[c, z, i, band(g), :], s_own.at[c, i])
+        return pltpu.make_async_copy(src.at[:, wide_cols(y, h)], qd.at[z, i, band(g), :], s_own.at[i])
 
     def own_kv(i):
         src = (key_cur, value_cur)[i]
@@ -529,28 +532,28 @@
             src.at[:, pl.ds(pl.multiple_of(y * part_w, HS), part_w)], kv.at[i, hist_rows(y), :], s_hist.at[i]
         )
 
-    def a_copy(c, k, i):
+    def a_copy(k, i):
         src = (query, d_out)[i]
         p, py, ph = peer(k)
         return copy(
-            src.at[:, cols(py, ph, c)], qd.at[c, z, i, band(g), :],
-            s_a.at[c, k - 1, i], r_a.at[c, k - 1, i], z * ny + py, ph,
-        )
-
-    def kv_copy(c, k, i):
+            src.at[:, wide_cols(py, ph)], qd.at[z, i, band(g), :],
+            s_a.at[k - 1, i], r_a.at[k - 1, i], z * ny + py, ph,
+        )
+
+    def kv_copy(k, i):
         src = (key_cur, value_cur)[i]
         p, py, ph = peer(k)
         return copy(
-            src.at[:, cols(py, ph, c)], kv.at[i, band(g), part(c)],
-            s_kv.at[c, k - 1, i], r_kv.at[c, k - 1, i], z * ny + py, ph,
-        )
-
-    def h_copy(c, k, i):
+            src.at[:, wide_cols(py, ph)], kv.at[i, band(g), :],
+            s_kv.at[k - 1, i], r_kv.at[k - 1, i], z * ny + py, ph,
+        )
+
+    def h_copy(k, i):
         src = (key_hist, value_hist)[i]
         py = (y + k) % ny
         return copy(
-            src.at[:, hist_cols(py, c)], kv.at[i, hist_rows(y), part(c)],
-            s_h.at[c, k - 1, i], r_h.at[c, k - 1, i], z * ny + py, h,
+            src.at[:, pl.ds(pl.multiple_of(py * part_w, HS), part_w)], kv.at[i, hist_rows(y), :],
+            s_h.at[k - 1, i], r_h.at[k - 1, i], z * ny + py, h,
         )
 
     def l_copy(k):
@@ -558,8 +561,7 @@
         return copy(lens.at[y], lens.at[y], s_l.at[k - 1], r_l.at[k - 1], z * ny + py, h)
 
     for i in range(2):
-        for c in range(nc):
-            own_copy(c, i).start()
+        own_copy(i).start()
         own_kv(i).start()
         hist_copy(i).start()
 
@@ -576,18 +578,15 @@
     for k in range(1, ny):
         l_copy(k).start()
 
-    def exchange(c, cc):
-        for i in range(2):
-            for k in range(1, ng):
-                a_copy(c, k, i).start()
-        for i in range(2):
-            for k in range(1, ng):
-                kv_copy(c, k, i).start()
-            for k in range(1, ny):
-                h_copy(c, k, i).start()
-        return cc
-
-    lax.fori_loop(0, nc, exchange, 0)
+    for i in range(2):
+        for k in range(1, ng):
+            a_copy(k, i).start()
+    for i in range(2):
+        for k in range(1, ny):
+            h_copy(k, i).start()
+        for k in range(1, ng):
+            kv_copy(k, i).start()
+
     st[...] = jnp.zeros_like(st)
     dkv[...] = jnp.zeros_like(dkv)
     for k in range(1, ny):
@@ -602,7 +601,7 @@
 
     def z_copy(c, zz, way, hop):
         to = jnp.clip(z + 1 - 2 * way, 0, NZ - 1)
-        return copy(qd.at[c, zz], qd.at[c, zz], s_z.at[c, way, hop], r_z.at[c, way, hop], to * ny + y, h)
+        return copy(qd.at[zz, :, :, part(c)], qd.at[zz, :, :, part(c)], s_z.at[c, way, hop], r_z.at[c, way, hop], to * ny + y, h)
 
     def st_copy(c, b):
         return copy(st.at[c, b], st_in.at[c, z], s_st.at[c, b], r_st.at[c, z], b * ny + y, h)
@@ -615,9 +614,9 @@
 
     def pass1(c, b):
         for i in range(hpc):
-            hc, lc = head_cols(c * hpc + i), slice(i * HS, (i + 1) * HS)
-            s = nt_dot(kv[0, :, hc], qd[c, b, 0, :, lc]) * scale2 + bias[...]
-            gs = nt_dot(kv[1, :, hc], qd[c, b, 1, :, lc])
+            hc = head_cols(c * hpc + i)
+            s = nt_dot(kv[0, :, hc], qd[b, 0, :, hc]) * scale2 + bias[...]
+            gs = nt_dot(kv[1, :, hc], qd[b, 1, :, hc])
             m = jnp.max(s, axis=0, keepdims=True)
             w = jnp.exp2(s - m)
             kept[c, b, 0, i] = w
@@ -631,10 +630,12 @@
             st_copy(c, b).start()
 
     def own_sends(c):
-        for i in range(2):
-            own_copy(c, i).wait()
-            for k in range(1, ng):
-                a_copy(c, k, i).wait_recv()
+        @pl.when(c == 0)
+        def _():
+            for i in range(2):
+                own_copy(i).wait()
+                for k in range(1, ng):
+                    a_copy(k, i).wait_recv()
 
         @pl.when(z + 1 < NZ)
         def _():
@@ -678,14 +679,14 @@
     def own_pass(step, e):
         c, hop, ok = event(step, e)
 
-        @pl.when(ok & (hop == 0))
+        @pl.when(ok & (hop == 0) & (c == 0))
         def _():
             for i in range(2):
                 for k in range(1, ng):
-                    kv_copy(c, k, i).wait_recv()
+                    kv_copy(k, i).wait_recv()
                 for k in range(1, ny):
-                    h_copy(c, k, i).wait_recv()
-            kt[part(c), :] = kv[0, :, part(c)].T
+                    h_copy(k, i).wait_recv()
+            kt[...] = kv[0].T
 
         def one(way, cc):
             zz, there = block_at(hop, way)
@@ -722,12 +723,12 @@
     def order(i):
         return jnp.where(z < NZ // 2, NZ - 1 - i, i)
 
-    def b_copy(c, k, i):
+    def b_copy(k, i):
         p, py, ph = peer(k)
         dst = (out_k, out_v)[i]
         return copy(
-            fkv.at[i, band(p), part(c)], dst.at[:, cols(y, h, c)],
-            s_b.at[c, k - 1, i], r_b.at[c, k - 1, i], z * ny + py, ph,
+            fkv.at[i, band(p), :], dst.at[:, wide_cols(y, h)],
+            s_b.at[k - 1, i], r_b.at[k - 1, i], z * ny + py, ph,
         )
 
     def hb_copy(c, k, i):
@@ -746,7 +747,7 @@
             d = order(n)
             for i in range(hpc):
                 hc, lc = head_cols(c * hpc + i), slice(i * HS, (i + 1) * HS)
-                q, do = qd[c, d, 0, :, lc], qd[c, d, 1, :, lc]
+                q, do = qd[d, 0, :, hc], qd[d, 1, :, hc]
 
                 def row(ref, r):
                     return ref[c, d, r * hpc + i : r * hpc + i + 1, :]
@@ -764,12 +765,16 @@
             fkv[i, :, part(c)] = dkv[i, :, part(c)].astype(jnp.bfloat16)
             for k in range(1, ny):
                 hb_copy(c, k, i).start()
-            for k in range(1, ng):
-                b_copy(c, k, i).start()
-            out = (out_k, out_v)[i]
-            out[:, cols(y, h, c)] = fkv[i, band(g), part(c)]
             out = (out_kh, out_vh)[i]
             out[:, hist_cols(y, c)] = fkv[i, hist_rows(y), part(c)]
+
+        @pl.when(c == nc - 1)
+        def _():
+            for i in range(2):
+                for k in range(1, ng):
+                    b_copy(k, i).start()
+                out = (out_k, out_v)[i]
+                out[:, wide_cols(y, h)] = fkv[i, band(g), :]
 
     def rz_copy(c, d, way):
         to = jnp.clip(z + (1 if way == 0 else -1), 0, NZ - 1)
@@ -859,14 +864,9 @@
     def finish(c, cc):
         for k in range(1, ng):
             c_copy(c, k).wait()
-            for i in range(2):
-                b_copy(c, k, i).wait()
-                a_copy(c, k, i).wait_send()
-                kv_copy(c, k, i).wait_send()
         for k in range(1, ny):
             for i in range(2):
                 hb_copy(c, k, i).wait()
-                h_copy(c, k, i).wait_send()
         for k in range(1, NZ):
             f_copy(c, k).wait_send()
             st_copy(c, (z + k) % NZ).wait_send()
@@ -904,6 +904,13 @@
 
     for k in range(1, ny):
         l_copy(k).wait_send()
+        for i in range(2):
+            h_copy(k, i).wait_send()
+    for k in range(1, ng):
+        for i in range(2):
+            b_copy(k, i).wait()
+            a_copy(k, i).wait_send()
+            kv_copy(k, i).wait_send()
     lax.fori_loop(0, nc, finish, 0)
 
 
@@ -943,7 +950,7 @@
             in_specs=[pl.BlockSpec(memory_space=pltpu.SMEM)] + [hbm] * 6,
             out_specs=(vmem,) * 5,
             scratch_shapes=[
-                pltpu.VMEM((nc, NZ, 2, cur, wide), bf),
+                pltpu.VMEM((NZ, 2, cur, part_w), bf),
                 pltpu.VMEM((2, n_k, part_w), bf),
                 pltpu.VMEM((2, n_k, part_w), f32),
                 pltpu.VMEM((nc, NZ, wide, cur), bf),
@@ -959,13 +966,13 @@
                 pltpu.VMEM((part_w, n_k), bf),
                 pltpu.VMEM((nc, NZ, 2, 1, n_k, cur), f32),
                 pltpu.VMEM((ny, SLOTS, cur), jnp.int32),
-                sems(nc, ng - 1, 2), sems(nc, ng - 1, 2), sems(nc, ng - 1, 2), sems(nc, ng - 1, 2),
+                sems(ng - 1, 2), sems(ng - 1, 2), sems(ng - 1, 2), sems(ng - 1, 2),
                 sems(nc, 2, NZ), sems(nc, 2, NZ),
                 sems(nc, NZ), sems(nc, NZ), sems(nc, NZ - 1), sems(nc, NZ - 1),
                 sems(nc, 2, NZ), sems(nc, 2, NZ),
-                sems(nc, ng - 1, 2), sems(nc, ng - 1, 2), sems(nc, ng - 1), sems(nc, ng - 1),
-                sems(nc, 2), sems(2), sems(2),
-                sems(nc, ny - 1, 2), sems(nc, ny - 1, 2), sems(nc, ny - 1, 2), sems(nc, ny - 1, 2),
+                sems(ng - 1, 2), sems(ng - 1, 2), sems(nc, ng - 1), sems(nc, ng - 1),
+                sems(2), sems(2), sems(2),
+                sems(ny - 1, 2), sems(ny - 1, 2), sems(nc, ny - 1, 2), sems(nc, ny - 1, 2),
                 sems(ny - 1), sems(ny - 1),
             ],
             compiler_params=pltpu.CompilerParams(

time: 96.8 us -> 102 us (1.054)
  Pallas kernels: 90.3 us -> 95.5 us
    pallas_call x1, Pallas kernels: 90.3 us -> 95.5 us  [shards(): pl.pallas_call(functools.partial(kernel_split, nt, nh, nc), out_shape=out...]
where the time goes in v7:
time: 102 us
  Pallas kernels  95.5 us (94%)
  local copies, waits for them, and re-layouts  4.91 us (5%)
  between operations  1.31 us (1%)
    pallas_call x1, Pallas kernels, shards(): pl.pallas_call(functools.partial(kernel_split, nt, nh, nc), out_shape=out...  95.5 us
    unnamed x13, local copies, waits for them, and re-layouts  4.91 us

profile of v7, /device:TPU:0, one launch (start us, length us, event | category | flops | bytes accessed | tf_op | source)
XLA Modules:
  0.0 101.7 jit_solution(16604237704703920999)
XLA Ops:
  1.3 95.5 %attention_backward_split.1 = (bf16[32,3072]{1,0:T(8,128)(2,1)}, bf16[32,3072]{1,0:T(8,128)(2,1)}, bf16[32,3072]{1,0:T(8,128)(2,1)}, bf16[256,768]{1,0:T(8,128)(2,1)}, bf16[256,768]{1,0:T(8,128)(2,1)}) custom-call(s32[1]{0:T(128)S(6)} %copy.17.hist_len, bf16[32,3072]{1,0:T(8,128)(2,1)} %query.1, bf16[32,3072]{1,0:T(8,128)(2,1)} %d_out.1, ...), custom_call_target="tpu_custom_call" | custom-call | tf_op jit(solution)/shard_map/attention_backward_split/pallas_call | solution.py:947
  96.8 0.0 copy-start.3
  96.8 0.0 copy-start.2
  96.8 1.7 %copy.18 = bf16[32,3072]{1,0:T(8,128)(2,1)} copy(bf16[32,3072]{1,0:T(8,128)(2,1)} %get-tuple-element.10) | data formatting | bytes 393216
  98.5 0.0 copy-done.3
  98.5 0.0 copy-start.1
  98.5 0.7 copy.19
  99.2 0.0 copy-done.2
  99.2 0.7 copy.20
  99.9 0.0 copy-done.1
  99.9 0.0 copy-start
  99.9 0.7 copy.21
  100.6 0.4 copy-done
  101.0 0.7 copy.22
Async XLA Ops:
  96.8 1.7 %copy-start.3 = (bf16[32,3072]{1,0:T(8,128)(2,1)S(1)}, bf16[32,3072]{1,0:T(8,128)(2,1)}, u32[]{:S(2)}) copy-start(bf16[32,3072]{1,0:T(8,128)(2,1)} %get-tuple-element.11) | copy-start | bytes 589828
  96.8 2.4 %copy-start.2 = (bf16[32,3072]{1,0:T(8,128)(2,1)S(1)}, bf16[32,3072]{1,0:T(8,128)(2,1)}, u32[]{:S(2)}) copy-start(bf16[32,3072]{1,0:T(8,128)(2,1)} %get-tuple-element.12) | copy-start | bytes 589828
  98.5 1.4 %copy-start.1 = (bf16[256,768]{1,0:T(8,128)(2,1)S(1)}, bf16[256,768]{1,0:T(8,128)(2,1)}, u32[]{:S(2)}) copy-start(bf16[256,768]{1,0:T(8,128)(2,1)} %get-tuple-element.13) | copy-start | bytes 1179652
  99.9 1.1 %copy-start = (bf16[256,768]{1,0:T(8,128)(2,1)S(1)}, bf16[256,768]{1,0:T(8,128)(2,1)}, u32[]{:S(2)}) copy-start(bf16[256,768]{1,0:T(8,128)(2,1)} %get-tuple-element.14) | copy-start | bytes 1179652

commit v8 on v6

--- a/solution.py
+++ b/solution.py
@@ -587,7 +587,7 @@
                 h_copy(c, k, i).start()
         return cc
 
-    lax.fori_loop(0, nc, exchange, 0)
+    exchange(0, 0)
     st[...] = jnp.zeros_like(st)
     dkv[...] = jnp.zeros_like(dkv)
     for k in range(1, ny):
@@ -826,6 +826,11 @@
             lax.fori_loop(0, 2, run, 0)
 
         each(forward, step)
+
+        @pl.when((step % 2 == 0) & (step // 2 + 1 < nc))
+        def _():
+            exchange(step // 2 + 1, 0)
+
         each(own_pass, step)
 
         half, odd = step // 2, step % 2

time: 96.8 us -> 93.9 us (0.970)
  Pallas kernels: 90.3 us -> 87.5 us
    pallas_call x1, Pallas kernels: 90.3 us -> 87.5 us  [shards(): pl.pallas_call(functools.partial(kernel_split, nt, nh, nc), out_shape=out...]
where the time goes in v8:
time: 93.9 us; the launch traced here: 93.7 us
  Pallas kernels  87.5 us (93%)
  local copies, waits for them, and re-layouts  4.91 us (5%)
  between operations  1.31 us (1%)
    pallas_call x1, Pallas kernels, shards(): pl.pallas_call(functools.partial(kernel_split, nt, nh, nc), out_shape=out...  87.5 us
    unnamed x13, local copies, waits for them, and re-layouts  4.91 us

profile of v8, /device:TPU:0, one launch (start us, length us, event | category | flops | bytes accessed | tf_op | source)
XLA Modules:
  0.0 93.7 jit_solution(3115644440144690359)
XLA Ops:
  1.3 87.5 %attention_backward_split.1 = (bf16[32,3072]{1,0:T(8,128)(2,1)}, bf16[32,3072]{1,0:T(8,128)(2,1)}, bf16[32,3072]{1,0:T(8,128)(2,1)}, bf16[256,768]{1,0:T(8,128)(2,1)}, bf16[256,768]{1,0:T(8,128)(2,1)}) custom-call(s32[1]{0:T(128)S(6)} %copy.17.hist_len, bf16[32,3072]{1,0:T(8,128)(2,1)} %query.1, bf16[32,3072]{1,0:T(8,128)(2,1)} %d_out.1, ...), custom_call_target="tpu_custom_call" | custom-call | tf_op jit(solution)/shard_map/attention_backward_split/pallas_call | solution.py:945
  88.8 0.0 copy-start.3
  88.8 0.0 copy-start.2
  88.8 1.7 %copy.18 = bf16[32,3072]{1,0:T(8,128)(2,1)} copy(bf16[32,3072]{1,0:T(8,128)(2,1)} %get-tuple-element.10) | data formatting | bytes 393216
  90.5 0.0 copy-done.3
  90.5 0.0 copy-start.1
  90.5 0.7 copy.19
  91.2 0.0 copy-done.2
  91.2 0.7 copy.20
  91.8 0.0 copy-done.1
  91.8 0.0 copy-start
  91.8 0.7 copy.21
  92.6 0.4 copy-done
  93.0 0.7 copy.22
Async XLA Ops:
  88.8 1.7 %copy-start.3 = (bf16[32,3072]{1,0:T(8,128)(2,1)S(1)}, bf16[32,3072]{1,0:T(8,128)(2,1)}, u32[]{:S(2)}) copy-start(bf16[32,3072]{1,0:T(8,128)(2,1)} %get-tuple-element.11) | copy-start | bytes 589828
  88.8 2.4 %copy-start.2 = (bf16[32,3072]{1,0:T(8,128)(2,1)S(1)}, bf16[32,3072]{1,0:T(8,128)(2,1)}, u32[]{:S(2)}) copy-start(bf16[32,3072]{1,0:T(8,128)(2,1)} %get-tuple-element.12) | copy-start | bytes 589828
  90.5 1.4 %copy-start.1 = (bf16[256,768]{1,0:T(8,128)(2,1)S(1)}, bf16[256,768]{1,0:T(8,128)(2,1)}, u32[]{:S(2)}) copy-start(bf16[256,768]{1,0:T(8,128)(2,1)} %get-tuple-element.13) | copy-start | bytes 1179652
  91.8 1.1 %copy-start = (bf16[256,768]{1,0:T(8,128)(2,1)S(1)}, bf16[256,768]{1,0:T(8,128)(2,1)}, u32[]{:S(2)}) copy-start(bf16[256,768]{1,0:T(8,128)(2,1)} %get-tuple-element.14) | copy-start | bytes 1179652
